TPU v7x, 128 devices: a whole 4x4x4 slice. The times are simulated.
128 devices in a mesh: space: 64 (over y, z, x), batch: 2 (over core).
Axes of the slice: x: 4, y: 4, z: 4, core: 2. Of those that a mesh axis runs over, the one named last changes fastest.
Arguments:
- volume: bfloat16 [4, 2, 256, 128, 128], P(None, 'batch', 'space'), may hold values from -72 to 72
- kernel_one: bfloat16 [108, 32], replicated, may hold values from -0.625 to 0.625
- kernel_two: bfloat16 [864, 64], replicated, may hold values from -0.21875 to 0.21875
- cotangent: bfloat16 [64, 2, 64, 1024], P(None, 'batch', 'space'), may hold values from -6 to 6
Outputs:
- features: bfloat16 [64, 2, 64, 1024], P(None, 'batch', None, 'space')
- factor_in_one: float32 [108, 108], replicated
- factor_in_two: float32 [864, 864], replicated
- factor_out_one: float32 [32, 32], replicated
- factor_out_two: float32 [64, 64], replicated
- weight_grad_one: float32 [108, 32], replicated
- weight_grad_two: float32 [864, 64], replicated
All inputs are finite; a program needn't handle non-finite values.
Results may differ from a plain program's by a relative error of at most 0.007.
Values may be sent and summed in bfloat16 or wider, within the bound.
A program may use at most 128 MiB of HBM per device.

v0:
```python
import math

import jax
import jax.numpy as jnp
import numpy as np
from jax import lax
from jax.experimental import pallas as pl
from jax.experimental.pallas import tpu as pltpu
from jax.sharding import PartitionSpec as P

F32 = jnp.float32
BF16 = jnp.bfloat16
VMEM_CAP = 56 * 1024 * 1024
TOTAL_ONE = 2 * 128 * 64 * 64
TOTAL_TWO = 2 * 64 * 32 * 32


def spread_matrix():
    table = np.zeros((4, 128, 5, 4, 32), np.float32)
    for m in range(4):
        for res in range(5):
            for x2 in range(32):
                x = 4 * x2 + res - 1
                if x >= 0:
                    table[m, x, res, m, x2] = 1
    return jnp.asarray(table.reshape(512, 640), BF16)


def tap_matrix():
    table = np.zeros((128, 4, 3, 128), np.float32)
    for p in range(2):
        for q in range(2):
            for c in range(4):
                for a in range(3):
                    for b in range(3):
                        for e in range(3):
                            row = c * 27 + a * 9 + b * 3 + e
                            table[row, p * 2 + q, a, (2 * q + e) * 20 + c * 5 + 2 * p + b] = 1
    return jnp.asarray(table.reshape(128, 1536), BF16)


def gelu_parts(value):
    square = value * value
    tangent = jnp.tanh(0.7978845608028654 * (value + 0.044715 * value * square))
    half = 0.5 * (1.0 + tangent)
    slope = half + 0.5 * value * (1.0 - tangent * tangent) * 0.7978845608028654 * (1.0 + 3.0 * 0.044715 * square)
    return value * half, slope


def dot(a, b):
    return lax.dot_general(a, b, (((1,), (0,)), ((), ())), preferred_element_type=F32)


def dot_nt(a, b):
    return lax.dot_general(a, b, (((1,), (1,)), ((), ())), preferred_element_type=F32)


def halves(value):
    high = value.astype(BF16)
    return high, (value - high.astype(F32)).astype(BF16)


def forward_kernel(
    vol_ref, rim_ref, k1_ref, k2_ref, cot_ref, spread_ref, tap_ref,
    sums_ref, feat_ref, g2_ref, u_ref, slope_ref,
    vf, lf, of, uu, k1p, ww, p2f, p2b, tiles,
):
    lane = lax.broadcasted_iota(jnp.int32, (1, 1024), 1)
    for zz in range(7):
        for c in range(4):
            plane = rim_ref[c, 0, zz] if zz < 3 else vol_ref[c, 0, zz - 3]
            vf[zz * 4 + c, 8:136, :] = plane.astype(F32)
            vf[zz * 4 + c, 0:8, :] = jnp.zeros((8, 128), F32)
    for plane in range(28):
        for res in range(5):
            for m in range(4):
                row = (plane * 5 + res) * 8
                lf[row : row + 8, m * 128 : (m + 1) * 128] = vf[plane, pl.ds(7 + 4 * m + res, 8, stride=16), :]
    spread = dot(lf[...].astype(BF16), spread_ref[...])
    for zz in range(7):
        for res in range(5):
            of[zz * 1024 + res * 160 : zz * 1024 + (res + 1) * 160, :] = spread[
                zz * 160 : (zz + 1) * 160, res * 128 : (res + 1) * 128
            ]
        of[zz * 1024 + 800 : zz * 1024 + 896, :] = jnp.zeros((96, 128), F32)
    for zz in range(7):
        for group in range(7):
            for j in range(8):
                start = zz * 1024 + group * 128 + j
                part = jnp.concatenate(
                    [of[pl.ds(start, 8, stride=8), :], of[pl.ds(start + 64, 8, stride=8), :]], axis=0
                )
                uu[zz * 128 + group * 16 : zz * 128 + (group + 1) * 16, j * 128 : (j + 1) * 128] = part.astype(BF16)
        uu[zz * 128 + 112 : zz * 128 + 128, :] = jnp.zeros((16, 1024), BF16)
    u_ref[...] = uu[256:896, :]

    k1p[...] = jnp.zeros((32, 128), BF16)
    k1p[:, 0:108] = k1_ref[...]
    wide = dot(k1p[...], tap_ref[...])
    for pq in range(4):
        ww[pq * 32 : (pq + 1) * 32, :] = wide[:, pq * 384 : (pq + 1) * 384].astype(BF16)

    for h in range(3):
        pre = dot(ww[...], uu[h * 256 : h * 256 + 384, :])
        act, slope = gelu_parts(pre)
        if h > 0:
            slope_ref[(h - 1) * 128 : h * 128, :] = slope
        act = act.astype(BF16).astype(F32)
        for b in range(3):
            for e in range(3):
                p, q = (b + 1) % 2, (e + 1) % 2
                block = act[(p * 2 + q) * 32 : (p * 2 + q + 1) * 32, :]
                if e == 0:
                    block = jnp.where(lane % 32 == 0, 0.0, pltpu.roll(block, 1, 1))
                if b == 0:
                    block = jnp.where(lane < 32, 0.0, pltpu.roll(block, 32, 1))
                tap = h * 9 + b * 3 + e
                for j in range(8):
                    p2f[j, pl.ds(tap, 32, stride=27), :] = block[:, j * 128 : (j + 1) * 128]
    for j in range(8):
        p2b[0:864, j * 128 : (j + 1) * 128] = p2f[j].astype(BF16)
    p2b[864:896, :] = jnp.zeros((32, 1024), BF16)
    p2b[896:1280, :] = p2b[0:384, :]

    pre_two = dot(k2_ref[...], p2b[0:864, :])
    act, slope = gelu_parts(pre_two)
    act = act.astype(BF16).astype(F32)
    g2 = (cot_ref[...].astype(F32) * (1.0 / math.sqrt(TOTAL_TWO)) * slope).astype(BF16)
    g2_ref[...] = g2

    chan = lax.broadcasted_iota(jnp.int32, (64, 1024), 0) % 8
    group = (lax.broadcasted_iota(jnp.int32, (64, 1024), 1) // 16) % 8
    for bit in (4, 2, 1):
        down = pltpu.roll(pltpu.roll(act, 64 - bit, 0), bit * 16, 1)
        up = pltpu.roll(pltpu.roll(act, bit, 0), 1024 - bit * 16, 1)
        in_chan = (chan & bit) != 0
        in_group = (group & bit) != 0
        act = jnp.where(in_chan == in_group, act, jnp.where(in_group, down, up))
    for r in range(8):
        for g in range(8):
            feat_ref[pl.ds(64 * g + r, 8, stride=8), :] = act[r * 8 : (r + 1) * 8, g * 128 : (g + 1) * 128]

    for i in range(7):
        block = dot_nt(p2b[i * 128 : (i + 1) * 128, :], p2b[i * 128 : i * 128 + 512, :]) * (1.0 / TOTAL_TWO)
        sums_ref[i * 128 : (i + 1) * 128, :] = block.astype(BF16)
    grads = dot_nt(g2, p2b[0:896, :])
    own = dot_nt(g2, g2)
    sums_ref[896:960, :] = grads[:, 0:512].astype(BF16)
    sums_ref[960:1024, 0:384] = grads[:, 512:896].astype(BF16)
    sums_ref[960:1024, 384:512] = jnp.concatenate([own, jnp.zeros((64, 64), F32)], axis=1).astype(BF16)
    gram = dot_nt(uu[256:640, :], uu[256:640, :]) + dot_nt(uu[512:896, :], uu[512:896, :])
    total = jnp.zeros((128, 128), F32)
    for part in halves(gram):
        for pq in range(4):
            taps = tap_ref[:, pq * 384 : (pq + 1) * 384]
            total = total + dot(taps, dot_nt(part, taps).astype(BF16))
    total = total * (1.0 / TOTAL_ONE)
    for k in range(4):
        tiles[:, k * 128 : (k + 1) * 128] = total[k * 32 : (k + 1) * 32, :]
    sums_ref[864:896, :] = tiles[...].astype(BF16)


def backward_kernel(u_ref, slope_ref, g2_ref, above_ref, k2_ref, tap_ref, late_ref, k2f, aa, gs):
    lane = lax.broadcasted_iota(jnp.int32, (1, 1024), 1)
    k2f[:, 0:64] = k2_ref[...].astype(F32).T
    aa[...] = jnp.zeros((3, 128, 256), BF16)
    for a in range(3):
        for b in range(3):
            for e in range(3):
                p, q = (b + 1) % 2, (e + 1) % 2
                sy, sx = int(b == 0), int(e == 0)
                block = k2f[pl.ds(a * 9 + b * 3 + e, 32, stride=27), :]
                at = (p * 2 + q) * 32
                aa[a, at : at + 32, (sy * 2 + sx) * 64 : (sy * 2 + sx + 1) * 64] = block[:, 0:64].astype(BF16)
    for n, ref in enumerate((g2_ref, above_ref)):
        for sy in range(2):
            for sx in range(2):
                moved = ref[...].astype(F32)
                if sx:
                    moved = jnp.where(lane % 32 == 31, 0.0, pltpu.roll(moved, 1023, 1))
                if sy:
                    moved = jnp.where(lane >= 992, 0.0, pltpu.roll(moved, 992, 1))
                gs[n, (sy * 2 + sx) * 64 : (sy * 2 + sx + 1) * 64, :] = moved.astype(BF16)
    cross = jnp.zeros((128, 384), F32)
    gram = jnp.zeros((128, 128), F32)
    for h in range(2):
        spread = dot(aa[h + 1], gs[0])
        if h == 1:
            spread = spread + dot(aa[0], gs[1])
        g1 = (spread * slope_ref[h * 128 : (h + 1) * 128, :]).astype(BF16)
        cross = cross + dot_nt(g1, u_ref[h * 256 : h * 256 + 384, :])
        gram = gram + dot_nt(g1, g1)
    weight = jnp.zeros((32, 128), F32)
    own = jnp.zeros((32, 32), F32)
    for pq in range(4):
        for part in halves(cross[pq * 32 : (pq + 1) * 32, :]):
            weight = weight + dot_nt(part, tap_ref[:, pq * 384 : (pq + 1) * 384])
        own = own + gram[pq * 32 : (pq + 1) * 32, pq * 32 : (pq + 1) * 32]
    late_ref[:, 0:128] = weight
    late_ref[:, 128:256] = jnp.concatenate([own, jnp.zeros((32, 96), F32)], axis=1)


def unpack_kernel(
    sums_ref, late_ref, feat_ref,
    features_ref, in_one_ref, in_two_ref, out_one_ref, out_two_ref, w_one_ref, w_two_ref,
):
    for i in range(7):
        rows = min(128, 864 - i * 128)
        for k in range(4):
            j = (i + k) % 7
            cols = min(128, 864 - j * 128)
            block = sums_ref[i * 128 : (i + 1) * 128, k * 128 : (k + 1) * 128].astype(F32)
            in_two_ref[i * 128 : i * 128 + rows, j * 128 : j * 128 + cols] = block[0:rows, 0:cols]
            if k:
                in_two_ref[j * 128 : j * 128 + cols, i * 128 : i * 128 + rows] = block.T[0:cols, 0:rows]
    w_two_ref[:, 0:512] = sums_ref[896:960, :].astype(F32)
    rest = sums_ref[960:1024, :].astype(F32)
    w_two_ref[:, 512:864] = rest[:, 0:352]
    out_two_ref[...] = rest[:, 384:448]
    first = sums_ref[864:896, :].astype(F32)
    for k in range(4):
        rows = min(32, 108 - k * 32)
        in_one_ref[k * 32 : k * 32 + rows, :] = first[0:rows, k * 128 : k * 128 + 108]
    late = late_ref[...]
    w_one_ref[...] = late[:, 0:108]
    out_one_ref[...] = late[:, 128:160]
    for r in range(8):
        block = feat_ref[pl.ds(r, 64, stride=8), :]
        features_ref[r * 8 : (r + 1) * 8, 0, :, :] = block.T.reshape(8, 16, 64).astype(BF16)


VM = pl.BlockSpec(memory_space=pltpu.VMEM)


def passed_along(block, axis, distance):
    devices = range(lax.axis_size(axis))
    route = [(i - distance, i) for i in devices if i - distance in devices]
    return lax.ppermute(block, axis, route)


def local(volume, kernel_one, kernel_two, cotangent):
    shape = jax.ShapeDtypeStruct
    spread, taps = spread_matrix(), tap_matrix()
    rim = passed_along(volume[:, :, 1:], "space", 1)
    sums, feat, g2, uu, slope = pl.pallas_call(
        forward_kernel,
        name="forward",
        out_shape=(
            shape((1024, 512), BF16), shape((512, 128), F32), shape((64, 1024), BF16),
            shape((640, 1024), BF16), shape((256, 1024), F32),
        ),
        in_specs=[VM] * 7,
        out_specs=(VM,) * 5,
        scratch_shapes=[
            pltpu.VMEM((28, 136, 128), F32),
            pltpu.VMEM((1120, 512), F32),
            pltpu.VMEM((7 * 1024, 128), F32),
            pltpu.VMEM((896, 1024), BF16),
            pltpu.VMEM((32, 128), BF16),
            pltpu.VMEM((128, 384), BF16),
            pltpu.VMEM((8, 864, 128), F32),
            pltpu.VMEM((1280, 1024), BF16),
            pltpu.VMEM((32, 512), F32),
        ],
        compiler_params=pltpu.CompilerParams(vmem_limit_bytes=VMEM_CAP),
    )(volume, rim, kernel_one.T, kernel_two.T, cotangent.reshape(64, 1024), spread, taps)
    above = passed_along(g2, "space", -1)
    late = pl.pallas_call(
        backward_kernel,
        name="backward",
        out_shape=shape((32, 256), F32),
        in_specs=[VM] * 6,
        out_specs=VM,
        scratch_shapes=[
            pltpu.VMEM((864, 128), F32),
            pltpu.VMEM((3, 128, 256), BF16),
            pltpu.VMEM((2, 256, 1024), BF16),
        ],
        compiler_params=pltpu.CompilerParams(vmem_limit_bytes=VMEM_CAP),
    )(uu, slope, g2, above, kernel_two.T, taps)
    feat = lax.all_to_all(feat, "space", split_axis=0, concat_axis=0, tiled=True)
    late, sums = lax.psum((late, sums.astype(F32)), ("space", "batch"))
    features, in_one, in_two, out_one, out_two, w_one, w_two = pl.pallas_call(
        unpack_kernel,
        name="unpack",
        out_shape=(
            shape((64, 1, 16, 64), BF16), shape((108, 108), F32), shape((864, 864), F32), shape((32, 32), F32),
            shape((64, 64), F32), shape((32, 108), F32), shape((64, 864), F32),
        ),
        in_specs=[VM] * 3,
        out_specs=(VM,) * 7,
        compiler_params=pltpu.CompilerParams(vmem_limit_bytes=VMEM_CAP),
    )(sums, late, feat)
    return features.transpose(0, 1, 3, 2), in_one, in_two, out_one, out_two, w_one.T, w_two.T


def solution(mesh):
    placed = (P(None, "batch", "space", None, None), P(), P(), P(None, "batch", "space", None))
    return jax.shard_map(
        local,
        mesh=mesh,
        in_specs=placed,
        out_specs=(P(None, "batch", None, "space"), P(), P(), P(), P(), P(), P()),
        check_vma=False,
    )
```

profile of v0, /device:TPU:1, one launch (start us, length us, event | category | flops | bytes accessed | tf_op | source)
XLA Modules:
  0.0 153.0 jit_solution(11025245104593974456)
XLA Ops:
  0.6 1.0 slice.3
  1.7 4.0 %collective-permute-start = (bf16[4,1,3,128,128]{4,3,2,1,0:T(8,128)(2,1)S(1)}, bf16[4,1,3,128,128]{4,3,2,1,0:T(8,128)(2,1)S(1)}, u32[]{:S(2)}, u32[]{:S(2)}) collective-permute-start(bf16[4,1,3,128,128]{4,3,2,1,0:T(8,128)(2,1)S(1)} %slice.3), channel_id=1, source_target_pairs={{0,2},{2,4},{4,6},{6,8},{8,10},{10,12},{12,14},{14,16},{16,18},{18... | collective-permute-start | bytes 1179656 | tf_op jit(solution)/shard_map/ppermute | solution.py:238
  5.6 7.7 %collective-permute-done.rim_ref = bf16[4,1,3,128,128]{4,3,2,1,0:T(8,128)(2,1)S(1)} collective-permute-done((bf16[4,1,3,128,128]{4,3,2,1,0:T(8,128)(2,1)S(1)}, bf16[4,1,3,128,128]{4,3,2,1,0:T(8,128)(2,1)S(1)}, u32[]{:S(2)}, u32[]{:S(2)}) %collective-permute-start) | collective-permute-done | bytes 393248 | tf_op jit(solution)/shard_map/ppermute | solution.py:238
  13.4 0.0 copy-start.2
  13.4 0.8 copy-done.2
  14.1 12.1 %forward.1 = (bf16[1024,512]{1,0:T(8,128)(2,1)}, f32[512,128]{1,0:T(8,128)}, bf16[64,1024]{1,0:T(8,128)(2,1)}, bf16[640,1024]{1,0:T(8,128)(2,1)}, f32[256,1024]{1,0:T(8,128)}) custom-call(bf16[4,1,4,128,128]{4,3,2,1,0:T(8,128)(2,1)} %vol_ref.1, bf16[4,1,3,128,128]{4,3,2,1,0:T(8,128)(2,1)} %copy-done.2, bf16[32,108]{1,0:T(8,128)(2,1)} %bitcast.13, ...), custom_call_target="tpu_custom_call" | custom-call | tf_op jit(solution)/shard_map/forward/pallas_call | solution.py:245
  26.3 0.0 copy-start.1
  26.3 1.4 collective-permute-start.1
  27.7 13.6 %all-to-all-start = ((f32[64,8,128]{2,1,0:T(8,128)}), f32[64,8,128]{2,1,0:T(8,128)S(1)}, u32[]{:S(2)}, u32[]{:S(2)}) async-start(f32[64,8,128]{2,1,0:T(8,128)} %bitcast.11), calls=%async_computation | async-start | bytes 524288 | tf_op jit(solution)/shard_map/all_to_all | solution.py:281
  41.3 0.0 collective-permute-done.1.above_ref
  41.3 0.0 copy-start.3
  41.3 0.6 copy-done.3
  41.9 4.1 %backward.1 = f32[32,256]{1,0:T(8,128)} custom-call(bf16[640,1024]{1,0:T(8,128)(2,1)} %get-tuple-element.20.u_ref, f32[256,1024]{1,0:T(8,128)} %get-tuple-element.21.slope_ref, bf16[64,1024]{1,0:T(8,128)(2,1)} %get-tuple-element.22.g2_ref, bf16[64,1024]{1,0:T(8,128)(2,1)} %copy-done.3, bf16[64,864]{1,0:T(8,128)(2,1)} %bitcast.10, ...), custom_call_target="tpu_custom_call" | custom-call | tf_op jit(solution)/shard_map/backward/pallas_call | solution.py:268
  46.0 0.0 copy-done.1
  46.1 102.3 %all-reduce.2 = (f32[1024,512]{1,0:T(8,128)}, f32[32,256]{1,0:T(8,128)}) all-reduce(bf16[1024,512]{1,0:T(8,128)(2,1)S(1)} %copy-done.1, f32[32,256]{1,0:T(8,128)} %backward.1), channel_id=1, replica_groups=mesh['space'=64,'batch'=2] {'space','batch'}, use_global_device_ids=true, to_apply=%region_0.0 | all-reduce | flops 532480 | bytes 3211264 | tf_op jit(solution)/shard_map/psum | solution.py:282
  148.4 0.0 all-to-all-done
  148.4 0.0 copy-start
  148.4 0.7 copy-done
  149.1 3.9 %unpack.1 = (bf16[64,1,16,64]{3,2,1,0:T(8,128)(2,1)}, f32[108,108]{1,0:T(8,128)}, f32[864,864]{1,0:T(8,128)}, f32[32,32]{1,0:T(8,128)}, f32[64,64]{1,0:T(8,128)}, /*index=5*/f32[32,108]{1,0:T(8,128)}, f32[64,864]{1,0:T(8,128)}) custom-call(f32[1024,512]{1,0:T(8,128)} %get-tuple-element.31.sums_ref, f32[32,256]{1,0:T(8,128)} %get-tuple-element.32.late_ref, ...), custom_call_target="tpu_custom_call" | custom-call | tf_op jit(solution)/shard_map/unpack/pallas_call | solution.py:283
Async XLA Ops:
  1.7 11.7 %collective-permute-start = (bf16[4,1,3,128,128]{4,3,2,1,0:T(8,128)(2,1)S(1)}, bf16[4,1,3,128,128]{4,3,2,1,0:T(8,128)(2,1)S(1)}, u32[]{:S(2)}, u32[]{:S(2)}) collective-permute-start(bf16[4,1,3,128,128]{4,3,2,1,0:T(8,128)(2,1)S(1)} %slice.3), channel_id=1, source_target_pairs={{0,2},{2,4},{4,6},{6,8},{8,10},{10,12},{12,14},{14,16},{16,18},{18... | collective-permute-start | bytes 1179656 | tf_op jit(solution)/shard_map/ppermute | solution.py:238
  13.4 0.8 copy-start.2
  26.3 19.8 %copy-start.1 = (bf16[1024,512]{1,0:T(8,128)(2,1)S(1)}, bf16[1024,512]{1,0:T(8,128)(2,1)}, u32[]{:S(2)}) copy-start(bf16[1024,512]{1,0:T(8,128)(2,1)} %get-tuple-element.19) | copy-start | bytes 3145732
  26.3 15.0 %collective-permute-start.1 = (bf16[64,1024]{1,0:T(8,128)(2,1)}, bf16[64,1024]{1,0:T(8,128)(2,1)S(1)}, u32[]{:S(2)}, u32[]{:S(2)}) collective-permute-start(bf16[64,1024]{1,0:T(8,128)(2,1)} %get-tuple-element.22.g2_ref), channel_id=1, source_target_pairs={{2,0},{4,2},{6,4},{8,6},{10,8},{12,10},{14,12},{16,14},{18,16},{20... | collective-permute-start | bytes 393224 | tf_op jit(solution)/shard_map/ppermute | solution.py:238
  27.7 120.7 %all-to-all-start = ((f32[64,8,128]{2,1,0:T(8,128)}), f32[64,8,128]{2,1,0:T(8,128)S(1)}, u32[]{:S(2)}, u32[]{:S(2)}) async-start(f32[64,8,128]{2,1,0:T(8,128)} %bitcast.11), calls=%async_computation | async-start | bytes 524288 | tf_op jit(solution)/shard_map/all_to_all | solution.py:281
  41.3 0.7 copy-start.3
  148.4 0.7 copy-start
where the time goes:
time: 154 us; the launch traced here: 153 us
  blocking collectives  102 us (66%)
  Pallas kernels  20.1 us (13%)
  starting transfers between devices  19 us (12%)
  waiting for transfers between devices  7.75 us (5%)
  local copies, waits for them, and re-layouts  3.14 us (2%)
    psum x1, blocking collectives, local(): late, sums = lax.psum((late, sums.astype(F32)), ('space', 'batch'))  102 us
    all_to_all x1, starting transfers between devices, local(): lax.all_to_all(feat, 'space', split_axis=0, concat_axis=0, tiled=True)  13.6 us
    pallas_call x1, Pallas kernels, local(): pl.pallas_call(forward_kernel, name='forward', out_shape=(shape((1024, 51...  12.1 us
    ppermute x2, waiting for transfers between devices, passed_along(): return lax.ppermute(block, axis, route)  7.74 us
    ppermute x2, starting transfers between devices, passed_along(): return lax.ppermute(block, axis, route)  5.38 us
    pallas_call x1, Pallas kernels, local(): pl.pallas_call(backward_kernel, name='backward', out_shape=shape((32, 256...  4.12 us
    pallas_call x1, Pallas kernels, local(): pl.pallas_call(unpack_kernel, name='unpack', out_shape=(shape((64, 1, 16,...  3.9 us
  transfers between devices with their start and end apart: 3, of which 1 were waited for; matrix products, arithmetic and copies ran while one was open for 0% of the time, Pallas kernels for 3%

commit v1 on v0

--- a/solution.py
+++ b/solution.py
@@ -230,6 +230,151 @@
 
 
 VM = pl.BlockSpec(memory_space=pltpu.VMEM)
+MESH = pl.DeviceIdType.MESH
+
+
+def shifted(me, k):
+    y = lax.rem(me // 16 + k // 16, 4)
+    z = lax.rem(lax.rem(me // 4, 4) + lax.rem(k // 4, 4), 4)
+    x = lax.rem(lax.rem(me, 4) + lax.rem(k, 4), 4)
+    return y * 16 + z * 4 + x
+
+
+def sum_kernel(
+    sums_ref, late_ref, feat_ref, out_ref, late_out_ref, feat_out_ref,
+    pair, half, got, late_pair, late_x, late_sum, late_yz, late_total,
+    pair_sem, late_pair_sem, rs_sem, feat_sem, x_sem, yz_sem, gather_send, gather_recv, back_sem,
+):
+    me, core = lax.axis_index("space"), lax.axis_index("batch")
+    sibling = (me, 1 - core)
+    mine = pl.ds(pl.multiple_of(core * 256, 256), 256)
+    other = pl.ds(pl.multiple_of((1 - core) * 256, 256), 256)
+
+    def rows(index):
+        return pl.ds(pl.multiple_of(index * 16, 16), 16)
+
+    def send(src, dst, sems, to):
+        copy = pltpu.make_async_remote_copy(
+            src_ref=src, dst_ref=dst, send_sem=sems.at[0], recv_sem=sems.at[1], device_id=to, device_id_type=MESH
+        )
+        copy.start()
+        return copy
+
+    def await_bytes(ref, sem):
+        pltpu.make_async_copy(ref, ref, sem).wait()
+
+    barrier = pltpu.get_barrier_semaphore()
+    pl.semaphore_signal(barrier, inc=1, device_id=sibling, device_id_type=MESH)
+
+    def greet(k, carry):
+        pl.semaphore_signal(barrier, inc=1, device_id=(shifted(me, k), core), device_id_type=MESH)
+        return carry
+
+    lax.fori_loop(1, 64, greet, 0)
+    pl.semaphore_wait(barrier, 64)
+
+    pair_copy = send(sums_ref.at[:, other], pair, pair_sem, sibling)
+    late_copy = send(late_ref, late_pair, late_pair_sem, sibling)
+    pair_copy.wait()
+    half[...] = (sums_ref[:, mine].astype(F32) + pair[...].astype(F32)).astype(BF16)
+
+    def scatter(k, carry):
+        to = shifted(me, k)
+        send(half.at[rows(to), :], got.at[rows(k - 1), :], rs_sem, (to, core))
+        return carry
+
+    lax.fori_loop(1, 64, scatter, 0)
+
+    late_copy.wait()
+    late_sum[...] = late_ref[...] + late_pair[...]
+
+    def along_x(k, carry):
+        send(late_sum, late_x.at[k - 1], x_sem, (shifted(me, k), core))
+        return carry
+
+    lax.fori_loop(1, 4, along_x, 0)
+
+    def hand_on(k, carry):
+        to = shifted(me, k)
+        there = pl.ds(pl.multiple_of(to * 8, 8), 8)
+        here = pl.ds(pl.multiple_of(me * 8, 8), 8)
+        send(feat_ref.at[there, :], feat_out_ref.at[here, :], feat_sem, (to, core))
+        return carry
+
+    lax.fori_loop(1, 64, hand_on, 0)
+
+    await_bytes(late_x, x_sem.at[0])
+    await_bytes(late_x, x_sem.at[1])
+    late_total[...] = late_sum[...] + (late_x[0] + late_x[1] + late_x[2])
+
+    def across(k, carry):
+        send(late_total, late_yz.at[k - 1], yz_sem, (shifted(me, 4 * k), core))
+        return carry
+
+    lax.fori_loop(1, 16, across, 0)
+
+    await_bytes(got, rs_sem.at[1])
+
+    def add(k, total):
+        return total + got[rows(k), :].astype(F32)
+
+    total = lax.fori_loop(0, 63, add, half[rows(me), :].astype(F32))
+    out_ref[rows(me), mine] = total.astype(BF16)
+
+    def gather(k, carry):
+        piece = out_ref.at[rows(me), mine]
+        copy = pltpu.make_async_remote_copy(
+            src_ref=piece, dst_ref=piece, send_sem=gather_send, recv_sem=gather_recv.at[k // 16],
+            device_id=(shifted(me, k), core), device_id_type=MESH,
+        )
+        copy.start()
+        return carry
+
+    lax.fori_loop(1, 64, gather, 0)
+
+    await_bytes(late_yz, yz_sem.at[0])
+    await_bytes(late_yz, yz_sem.at[1])
+    late_out_ref[...] = lax.fori_loop(0, 15, lambda k, total: total + late_yz[k], late_total[...])
+    feat_out_ref[pl.ds(pl.multiple_of(me * 8, 8), 8), :] = feat_ref[pl.ds(pl.multiple_of(me * 8, 8), 8), :]
+
+    backs = []
+    for k in range(4):
+        count = 240 if k == 0 else 256
+        await_bytes(half.at[0:count, :], gather_recv.at[k])
+        block = pl.ds(pl.multiple_of(lax.rem(me // 16 + 4 - k, 4) * 256, 256), 256)
+        backs.append(send(out_ref.at[block, mine], out_ref.at[block, mine], back_sem.at[k], sibling))
+    for copy in backs:
+        copy.wait()
+    await_bytes(got, rs_sem.at[0])
+    await_bytes(got, gather_send)
+    for sem in (feat_sem.at[0], feat_sem.at[1]):
+        await_bytes(feat_out_ref.at[0:504, :], sem)
+
+
+def summed(sums, late, feat):
+    shape = jax.ShapeDtypeStruct
+    dma = pltpu.SemaphoreType.DMA
+    return pl.pallas_call(
+        sum_kernel,
+        name="summed",
+        out_shape=(shape((1024, 512), BF16), shape((32, 256), F32), shape((512, 128), F32)),
+        in_specs=[VM] * 3,
+        out_specs=(VM,) * 3,
+        scratch_shapes=[
+            pltpu.VMEM((1024, 256), BF16),
+            pltpu.VMEM((1024, 256), BF16),
+            pltpu.VMEM((1008, 256), BF16),
+            pltpu.VMEM((32, 256), F32),
+            pltpu.VMEM((3, 32, 256), F32),
+            pltpu.VMEM((32, 256), F32),
+            pltpu.VMEM((15, 32, 256), F32),
+            pltpu.VMEM((32, 256), F32),
+            dma((2,)), dma((2,)), dma((2,)), dma((2,)), dma((2,)), dma((2,)), dma, dma((4,)), dma((4, 2)),
+        ],
+        compiler_params=pltpu.CompilerParams(
+            vmem_limit_bytes=VMEM_CAP, collective_id=0, has_side_effects=True
+        ),
+    )(sums, late, feat)
 
 
 def passed_along(block, axis, distance):
@@ -278,8 +423,7 @@
         ],
         compiler_params=pltpu.CompilerParams(vmem_limit_bytes=VMEM_CAP),
     )(uu, slope, g2, above, kernel_two.T, taps)
-    feat = lax.all_to_all(feat, "space", split_axis=0, concat_axis=0, tiled=True)
-    late, sums = lax.psum((late, sums.astype(F32)), ("space", "batch"))
+    sums, late, feat = summed(sums, late, feat)
     features, in_one, in_two, out_one, out_two, w_one, w_two = pl.pallas_call(
         unpack_kernel,
         name="unpack",

time: 154 us -> 88.2 us (0.57)
  blocking collectives: 102 us -> 0 us
  Pallas kernels: 20.1 us -> 66.5 us
  starting transfers between devices: 19 us -> 5.25 us
  waiting for transfers between devices: 7.75 us -> 13.1 us
    psum x1 -> x0, blocking collectives: 102 us -> none  [local(): late, sums = lax.psum((late, sums.astype(F32)), ('space', 'batch'))]
    pallas_call x0 -> x1, Pallas kernels: none -> 46.8 us  [summed(): pl.pallas_call(sum_kernel, name='summed', out_shape=(shape((1024, 512), B...]
    all_to_all x1 -> x0, starting transfers between devices: 13.6 us -> none  [local(): lax.all_to_all(feat, 'space', split_axis=0, concat_axis=0, tiled=True)]
    ppermute x2, waiting for transfers between devices: 7.74 us -> 13.1 us  [passed_along(): return lax.ppermute(block, axis, route)]
  transfers between devices with their start and end apart: 3 -> 2, of which waited for: 1 -> 2; matrix products, arithmetic and copies ran while one was open for 0% -> 0% of each run, Pallas kernels for 3% -> 0%
where the time goes in v1:
time: 88.2 us; the launch traced here: 87.9 us
  Pallas kernels  66.5 us (75%)
  waiting for transfers between devices  13.1 us (15%)
  starting transfers between devices  5.25 us (6%)
  local copies, waits for them, and re-layouts  2.43 us (3%)
    pallas_call x1, Pallas kernels, summed(): pl.pallas_call(sum_kernel, name='summed', out_shape=(shape((1024, 512), B...  46.8 us
    ppermute x2, waiting for transfers between devices, passed_along(): return lax.ppermute(block, axis, route)  13.1 us
    pallas_call x1, Pallas kernels, local(): pl.pallas_call(forward_kernel, name='forward', out_shape=(shape((1024, 51...  12.1 us
    ppermute x2, starting transfers between devices, passed_along(): return lax.ppermute(block, axis, route)  5.25 us
    pallas_call x1, Pallas kernels, local(): pl.pallas_call(backward_kernel, name='backward', out_shape=shape((32, 256...  4.12 us
    pallas_call x1, Pallas kernels, local(): pl.pallas_call(unpack_kernel, name='unpack', out_shape=(shape((64, 1, 16,...  3.44 us
  transfers between devices with their start and end apart: 2, of which 2 were waited for; matrix products, arithmetic and copies ran while one was open for 0% of the time, Pallas kernels for 0%

profile of v1, /device:TPU:1, one launch (start us, length us, event | category | flops | bytes accessed | tf_op | source)
XLA Modules:
  0.0 87.9 jit_solution(18020955828707441472)
XLA Ops:
  0.6 1.0 %slice.3 = bf16[4,1,3,128,128]{4,3,2,1,0:T(8,128)(2,1)S(1)} slice(bf16[4,1,4,128,128]{4,3,2,1,0:T(8,128)(2,1)} %vol_ref.1), slice={[0:4], [0:1], [1:4], [0:128], [0:128]} | slice | bytes 786432 | tf_op jit(solution)/shard_map/slice | solution.py:389
  1.7 4.0 %collective-permute-start = (bf16[4,1,3,128,128]{4,3,2,1,0:T(8,128)(2,1)S(1)}, bf16[4,1,3,128,128]{4,3,2,1,0:T(8,128)(2,1)S(1)}, u32[]{:S(2)}, u32[]{:S(2)}) collective-permute-start(bf16[4,1,3,128,128]{4,3,2,1,0:T(8,128)(2,1)S(1)} %slice.3), channel_id=1, source_target_pairs={{0,2},{2,4},{4,6},{6,8},{8,10},{10,12},{12,14},{14,16},{16,18},{18... | collective-permute-start | bytes 1179656 | tf_op jit(solution)/shard_map/ppermute | solution.py:383
  5.6 7.7 %collective-permute-done.rim_ref = bf16[4,1,3,128,128]{4,3,2,1,0:T(8,128)(2,1)S(1)} collective-permute-done((bf16[4,1,3,128,128]{4,3,2,1,0:T(8,128)(2,1)S(1)}, bf16[4,1,3,128,128]{4,3,2,1,0:T(8,128)(2,1)S(1)}, u32[]{:S(2)}, u32[]{:S(2)}) %collective-permute-start) | collective-permute-done | bytes 393248 | tf_op jit(solution)/shard_map/ppermute | solution.py:383
  13.4 0.0 copy-start
  13.4 0.7 copy-done
  14.1 12.1 %forward.1 = (bf16[1024,512]{1,0:T(8,128)(2,1)}, f32[512,128]{1,0:T(8,128)}, bf16[64,1024]{1,0:T(8,128)(2,1)}, bf16[640,1024]{1,0:T(8,128)(2,1)}, f32[256,1024]{1,0:T(8,128)}) custom-call(bf16[4,1,4,128,128]{4,3,2,1,0:T(8,128)(2,1)} %vol_ref.1, bf16[4,1,3,128,128]{4,3,2,1,0:T(8,128)(2,1)} %copy-done, bf16[32,108]{1,0:T(8,128)(2,1)} %bitcast.9, ...), custom_call_target="tpu_custom_call" | custom-call | tf_op jit(solution)/shard_map/forward/pallas_call | solution.py:390
  26.2 1.3 %collective-permute-start.1 = (bf16[64,1024]{1,0:T(8,128)(2,1)}, bf16[64,1024]{1,0:T(8,128)(2,1)S(1)}, u32[]{:S(2)}, u32[]{:S(2)}) collective-permute-start(bf16[64,1024]{1,0:T(8,128)(2,1)} %get-tuple-element.25.g2_ref), channel_id=1, source_target_pairs={{2,0},{4,2},{6,4},{8,6},{10,8},{12,10},{14,12},{16,14},{18,16},{20... | collective-permute-start | bytes 393224 | tf_op jit(solution)/shard_map/ppermute | solution.py:383
  27.5 5.4 %collective-permute-done.1.above_ref = bf16[64,1024]{1,0:T(8,128)(2,1)S(1)} collective-permute-done((bf16[64,1024]{1,0:T(8,128)(2,1)}, bf16[64,1024]{1,0:T(8,128)(2,1)S(1)}, u32[]{:S(2)}, u32[]{:S(2)}) %collective-permute-start.1) | collective-permute-done | bytes 131104 | tf_op jit(solution)/shard_map/ppermute | solution.py:383
  32.9 0.0 copy-start.1
  32.9 0.6 copy-done.1
  33.6 4.1 %backward.1.late_ref = f32[32,256]{1,0:T(8,128)} custom-call(bf16[640,1024]{1,0:T(8,128)(2,1)} %get-tuple-element.23.u_ref, f32[256,1024]{1,0:T(8,128)} %get-tuple-element.24.slope_ref, bf16[64,1024]{1,0:T(8,128)(2,1)} %get-tuple-element.25.g2_ref, bf16[64,1024]{1,0:T(8,128)(2,1)} %copy-done.1, bf16[64,864]{1,0:T(8,128)(2,1)} %bitcast.7, ...), custom_call_target="tpu_custom_call" | custom-call | tf_op jit(solution)/shard_map/backward/pallas_call | solution.py:413
  37.7 46.8 %summed.1 = (bf16[1024,512]{1,0:T(8,128)(2,1)}, f32[32,256]{1,0:T(8,128)}, f32[512,128]{1,0:T(8,128)}) custom-call(bf16[1024,512]{1,0:T(8,128)(2,1)} %get-tuple-element.22.sums_ref, f32[32,256]{1,0:T(8,128)} %backward.1.late_ref, f32[512,128]{1,0:T(8,128)} %get-tuple-element.26.feat_ref), custom_call_target="tpu_custom_call" | custom-call | tf_op jit(solution)/shard_map/summed/pallas_call | solution.py:357
  84.5 3.4 %unpack.1 = (bf16[64,1,16,64]{3,2,1,0:T(8,128)(2,1)}, f32[108,108]{1,0:T(8,128)}, f32[864,864]{1,0:T(8,128)}, f32[32,32]{1,0:T(8,128)}, f32[64,64]{1,0:T(8,128)}, /*index=5*/f32[32,108]{1,0:T(8,128)}, f32[64,864]{1,0:T(8,128)}) custom-call(bf16[1024,512]{1,0:T(8,128)(2,1)} %get-tuple-element.27.sums_ref, f32[32,256]{1,0:T(8,128)} %get-tuple-element.28.late_ref, ...), custom_call_target="tpu_custom_call" | custom-call | tf_op jit(solution)/shard_map/unpack/pallas_call | solution.py:427
Async XLA Ops:
  1.7 11.7 %collective-permute-start = (bf16[4,1,3,128,128]{4,3,2,1,0:T(8,128)(2,1)S(1)}, bf16[4,1,3,128,128]{4,3,2,1,0:T(8,128)(2,1)S(1)}, u32[]{:S(2)}, u32[]{:S(2)}) collective-permute-start(bf16[4,1,3,128,128]{4,3,2,1,0:T(8,128)(2,1)S(1)} %slice.3), channel_id=1, source_target_pairs={{0,2},{2,4},{4,6},{6,8},{8,10},{10,12},{12,14},{14,16},{16,18},{18... | collective-permute-start | bytes 1179656 | tf_op jit(solution)/shard_map/ppermute | solution.py:383
  13.4 0.8 copy-start
  26.2 6.7 %collective-permute-start.1 = (bf16[64,1024]{1,0:T(8,128)(2,1)}, bf16[64,1024]{1,0:T(8,128)(2,1)S(1)}, u32[]{:S(2)}, u32[]{:S(2)}) collective-permute-start(bf16[64,1024]{1,0:T(8,128)(2,1)} %get-tuple-element.25.g2_ref), channel_id=1, source_target_pairs={{2,0},{4,2},{6,4},{8,6},{10,8},{12,10},{14,12},{16,14},{18,16},{20... | collective-permute-start | bytes 393224 | tf_op jit(solution)/shard_map/ppermute | solution.py:383
  32.9 0.6 copy-start.1

commit v2 on v0

v2 whole, which is shorter than its diff:
```python
import math

import jax
import jax.numpy as jnp
import numpy as np
from jax import lax
from jax.experimental import pallas as pl
from jax.experimental.pallas import tpu as pltpu
from jax.sharding import PartitionSpec as P

F32 = jnp.float32
BF16 = jnp.bfloat16
VMEM_CAP = 56 * 1024 * 1024
TOTAL_ONE = 2 * 128 * 64 * 64
TOTAL_TWO = 2 * 64 * 32 * 32


def tap_matrix():
    table = np.zeros((128, 4, 3, 128), np.float32)
    for p in range(2):
        for q in range(2):
            for c in range(4):
                for a in range(3):
                    for b in range(3):
                        for e in range(3):
                            row = c * 27 + a * 9 + b * 3 + e
                            table[row, p * 2 + q, a, (2 * q + e) * 20 + c * 5 + 2 * p + b] = 1
    return jnp.asarray(table.reshape(128, 1536), F32)


def gelu_parts(value):
    square = value * value
    tangent = jnp.tanh(0.7978845608028654 * (value + 0.044715 * value * square))
    half = 0.5 * (1.0 + tangent)
    slope = half + 0.5 * value * (1.0 - tangent * tangent) * 0.7978845608028654 * (1.0 + 3.0 * 0.044715 * square)
    return value * half, slope


def dot(a, b):
    return lax.dot_general(a, b, (((1,), (0,)), ((), ())), preferred_element_type=F32)


def dot_nt(a, b):
    return lax.dot_general(a, b, (((1,), (1,)), ((), ())), preferred_element_type=F32)


def halves(value):
    high = value.astype(BF16)
    return high, (value - high.astype(F32)).astype(BF16)


VM = pl.BlockSpec(memory_space=pltpu.VMEM)
MESH = pl.DeviceIdType.MESH


def shifted(me, k):
    y = lax.rem(me // 16 + k // 16, 4)
    z = lax.rem(lax.rem(me // 4, 4) + lax.rem(k // 4, 4), 4)
    x = lax.rem(lax.rem(me, 4) + lax.rem(k, 4), 4)
    return y * 16 + z * 4 + x


def rows(index, count=16):
    return pl.ds(pl.multiple_of(index * count, count), count)


def await_bytes(ref, sem):
    pltpu.make_async_copy(ref, ref, sem).wait()


def spread_planes(first, count, load, vf, lf, of, uu, ee):
    def split(zz, carry):
        for c in range(4):
            at = zz * 4 + c
            vf[at, 8:136, :] = load(c, zz)
            for res in range(5):
                row = pl.ds(pl.multiple_of(at * 40 + res * 8, 8), 8)
                for m in range(4):
                    lf[row, m * 128 : (m + 1) * 128] = vf[at, pl.ds(7 + 4 * m + res, 8, stride=16), :]
        return carry

    lax.fori_loop(0, count, split, 0)
    parts = dot(lf[0 : count * 160, :].astype(BF16), ee[...])
    for zz in range(count):
        for res in range(5):
            of[zz * 1024 + res * 160 : zz * 1024 + (res + 1) * 160, :] = parts[
                zz * 160 : (zz + 1) * 160, res * 128 : (res + 1) * 128
            ]

    def flatten(zz, carry):
        for group in range(7):
            for j in range(8):
                start = zz * 1024 + group * 128 + j
                part = jnp.concatenate(
                    [of[pl.ds(start, 8, stride=8), :], of[pl.ds(start + 64, 8, stride=8), :]], axis=0
                )
                at = pl.ds(pl.multiple_of((first + zz) * 128 + group * 16, 16), 16)
                uu[at, j * 128 : (j + 1) * 128] = part.astype(BF16)
        uu[pl.ds(pl.multiple_of((first + zz) * 128 + 112, 16), 16), :] = jnp.zeros((16, 1024), BF16)
        return carry

    lax.fori_loop(0, count, flatten, 0)


def place_taps(act, a, p2f):
    lane = lax.broadcasted_iota(jnp.int32, (1, 1024), 1)
    for b in range(3):
        for e in range(3):
            p, q = (b + 1) % 2, (e + 1) % 2
            block = act[(p * 2 + q) * 32 : (p * 2 + q + 1) * 32, :]
            if e == 0:
                block = jnp.where(lane % 32 == 0, 0.0, pltpu.roll(block, 1, 1))
            if b == 0:
                block = jnp.where(lane < 32, 0.0, pltpu.roll(block, 32, 1))
            for j in range(8):
                p2f[j, pl.ds(a * 9 + b * 3 + e, 32, stride=27), :] = block[:, j * 128 : (j + 1) * 128]


def first_factor(uu, taps, tiles):
    gram = dot_nt(uu[0:384, :], uu[0:384, :]) + dot_nt(uu[256:640, :], uu[256:640, :])
    total = jnp.zeros((128, 128), F32)
    for part in halves(gram):
        for pq in range(4):
            tap = taps[:, pq * 384 : (pq + 1) * 384]
            total = total + dot(tap, dot_nt(part, tap).astype(BF16))
    total = total * (1.0 / TOTAL_ONE)
    for k in range(4):
        tiles[:, k * 128 : (k + 1) * 128] = total[k * 32 : (k + 1) * 32, :]


def swap_groups(act):
    chan = lax.broadcasted_iota(jnp.int32, (64, 1024), 0) % 8
    group = (lax.broadcasted_iota(jnp.int32, (64, 1024), 1) // 16) % 8
    for bit in (4, 2, 1):
        down = pltpu.roll(pltpu.roll(act, 64 - bit, 0), bit * 16, 1)
        up = pltpu.roll(pltpu.roll(act, bit, 0), 1024 - bit * 16, 1)
        in_chan = (chan & bit) != 0
        in_group = (group & bit) != 0
        act = jnp.where(in_chan == in_group, act, jnp.where(in_group, down, up))
    return act


def backward_weights(k2_ref, k2f, aa):
    k2f[:, 0:64] = k2_ref[...].astype(F32).T
    aa[...] = jnp.zeros((3, 128, 256), BF16)
    for a in range(3):
        for b in range(3):
            for e in range(3):
                p, q = (b + 1) % 2, (e + 1) % 2
                sy, sx = int(b == 0), int(e == 0)
                block = k2f[pl.ds(a * 9 + b * 3 + e, 32, stride=27), :]
                at = (p * 2 + q) * 32
                aa[a, at : at + 32, (sy * 2 + sx) * 64 : (sy * 2 + sx + 1) * 64] = block[:, 0:64].astype(BF16)


def shift_back(value, gs, n):
    lane = lax.broadcasted_iota(jnp.int32, (1, 1024), 1)
    for sy in range(2):
        for sx in range(2):
            moved = value
            if sx:
                moved = jnp.where(lane % 32 == 31, 0.0, pltpu.roll(moved, 1023, 1))
            if sy:
                moved = jnp.where(lane >= 992, 0.0, pltpu.roll(moved, 992, 1))
            gs[n, (sy * 2 + sx) * 64 : (sy * 2 + sx + 1) * 64, :] = moved.astype(BF16)


def step_kernel(
    vol_ref, k1_ref, k2_ref, cot_ref, tap_ref, out_ref, late_out_ref, feat_out_ref,
    vf, lf, of, uu, ee, taps, k1p, ww, slopes, hid, p2f, p2b, tiles, sums, feat, g2, k2f, aa, gs,
    rim, hid_in, g2_in, pair, half, got, late, late_pair, late_x, late_sum, late_yz, late_total,
    rim_sem, hid_sem, g2_sem, pair_sem, late_pair_sem, rs_sem, feat_sem, x_sem, yz_sem,
    gather_send, gather_recv, back_sem,
):
    me, core = lax.axis_index("space"), lax.axis_index("batch")
    sibling = (me, 1 - core)
    above, below = (lax.rem(me + 1, 64), core), (lax.rem(me + 63, 64), core)
    mine = pl.ds(pl.multiple_of(core * 256, 256), 256)
    other = pl.ds(pl.multiple_of((1 - core) * 256, 256), 256)

    def send(src, dst, sems, to):
        copy = pltpu.make_async_remote_copy(
            src_ref=src, dst_ref=dst, send_sem=sems.at[0], recv_sem=sems.at[1], device_id=to, device_id_type=MESH
        )
        copy.start()
        return copy

    barrier = pltpu.get_barrier_semaphore()
    pl.semaphore_signal(barrier, inc=1, device_id=sibling, device_id_type=MESH)

    def greet(k, carry):
        pl.semaphore_signal(barrier, inc=1, device_id=(shifted(me, k), core), device_id_type=MESH)
        return carry

    lax.fori_loop(1, 64, greet, 0)

    at_x = lax.broadcasted_iota(jnp.int32, (128, 128), 0)
    lane = lax.broadcasted_iota(jnp.int32, (128, 128), 1)
    for m in range(4):
        for res in range(5):
            hit = (at_x == 4 * (lane - 32 * m) + (res - 1)) & (lane >= 32 * m) & (lane < 32 * (m + 1))
            ee[m * 128 : (m + 1) * 128, res * 128 : (res + 1) * 128] = jnp.where(hit, 1.0, 0.0).astype(BF16)
    vf[:, 0:8, :] = jnp.zeros((16, 8, 128), F32)
    for zz in range(4):
        of[zz * 1024 + 800 : zz * 1024 + 896, :] = jnp.zeros((96, 128), F32)
    taps[...] = tap_ref[...].astype(BF16)
    k1p[...] = jnp.zeros((32, 128), BF16)
    k1p[:, 0:108] = k1_ref[...]
    wide = dot(k1p[...], taps[...])
    for pq in range(4):
        ww[pq * 32 : (pq + 1) * 32, :] = wide[:, pq * 384 : (pq + 1) * 384].astype(BF16)

    spread_planes(1, 4, lambda c, zz: vol_ref[c, 0, zz].astype(F32), vf, lf, of, uu, ee)
    pl.semaphore_wait(barrier, 64)
    rim_copy = send(vol_ref.at[:, 0, 3], rim, rim_sem, above)
    act, slope = gelu_parts(dot(ww[...], uu[256:640, :]))
    slopes[128:256, :] = slope
    hid[...] = act.astype(BF16)
    hid_copy = send(hid, hid_in, hid_sem, above)
    place_taps(hid[...].astype(F32), 2, p2f)
    backward_weights(k2_ref, k2f, aa)

    rim_copy.wait()
    spread_planes(
        0, 1, lambda c, zz: jnp.where(me > 0, rim[c].astype(F32), 0.0), vf, lf, of, uu, ee
    )
    act, slope = gelu_parts(dot(ww[...], uu[0:384, :]))
    slopes[0:128, :] = slope
    place_taps(act.astype(BF16).astype(F32), 1, p2f)
    first_factor(uu, taps, tiles)

    hid_copy.wait()
    place_taps(jnp.where(me > 0, hid_in[...].astype(F32), 0.0), 0, p2f)
    for j in range(8):
        p2b[0:864, j * 128 : (j + 1) * 128] = p2f[j].astype(BF16)
    p2b[864:896, :] = jnp.zeros((32, 1024), BF16)
    p2b[896:1280, :] = p2b[0:384, :]
    act, slope = gelu_parts(dot(k2_ref[...], p2b[0:864, :]))
    g2[...] = (cot_ref[...].astype(F32) * (1.0 / math.sqrt(TOTAL_TWO)) * slope).astype(BF16)
    g2_copy = send(g2, g2_in, g2_sem, below)
    pre_act = act.astype(BF16).astype(F32)

    pairs = []

    def swap_block(i):
        block = slice(i * 128, (i + 1) * 128)
        pairs.append(send(sums.at[block, other], pair.at[block, :], pair_sem.at[i], sibling))

    grads = dot_nt(g2[...], p2b[0:896, :])
    own = dot_nt(g2[...], g2[...])
    sums[896:960, :] = grads[:, 0:512].astype(BF16)
    sums[960:1024, 0:384] = grads[:, 512:896].astype(BF16)
    sums[960:1024, 384:512] = jnp.concatenate([own, jnp.zeros((64, 64), F32)], axis=1).astype(BF16)
    swap_block(7)
    for i in (6, 0, 1, 2, 3, 4, 5):
        block = dot_nt(p2b[i * 128 : (i + 1) * 128, :], p2b[i * 128 : i * 128 + 512, :]) * (1.0 / TOTAL_TWO)
        sums[i * 128 : (i + 1) * 128, :] = block.astype(BF16)
        if i == 6:
            sums[864:896, :] = tiles[...].astype(BF16)
        swap_block(i)
    for n, i in enumerate((7, 6, 0, 1, 2, 3, 4, 5)):
        block = slice(i * 128, (i + 1) * 128)
        pairs[n].wait()
        half[block, :] = (sums[block, mine].astype(F32) + pair[block, :].astype(F32)).astype(BF16)

    def scatter(k, carry):
        to = shifted(me, k)
        send(half.at[rows(to), :], got.at[rows(k - 1), :], rs_sem, (to, core))
        return carry

    lax.fori_loop(1, 64, scatter, 0)

    moved = swap_groups(pre_act)
    for r in range(8):
        for g in range(8):
            feat[pl.ds(64 * g + r, 8, stride=8), :] = moved[r * 8 : (r + 1) * 8, g * 128 : (g + 1) * 128]

    def hand_on(k, carry):
        to = shifted(me, k)
        send(feat.at[rows(to, 8), :], feat_out_ref.at[rows(me, 8), :], feat_sem, (to, core))
        return carry

    lax.fori_loop(1, 64, hand_on, 0)
    feat_out_ref[rows(me, 8), :] = feat[rows(me, 8), :]

    shift_back(g2[...].astype(F32), gs, 0)
    g2_copy.wait()
    shift_back(jnp.where(me < 63, g2_in[...].astype(F32), 0.0), gs, 1)
    cross = jnp.zeros((128, 384), F32)
    gram = jnp.zeros((128, 128), F32)
    for h in range(2):
        spread = dot(aa[h + 1], gs[0])
        if h == 1:
            spread = spread + dot(aa[0], gs[1])
        g1 = (spread * slopes[h * 128 : (h + 1) * 128, :]).astype(BF16)
        cross = cross + dot_nt(g1, uu[h * 256 : h * 256 + 384, :])
        gram = gram + dot_nt(g1, g1)
    weight = jnp.zeros((32, 128), F32)
    own = jnp.zeros((32, 32), F32)
    for pq in range(4):
        for part in halves(cross[pq * 32 : (pq + 1) * 32, :]):
            weight = weight + dot_nt(part, taps[:, pq * 384 : (pq + 1) * 384])
        own = own + gram[pq * 32 : (pq + 1) * 32, pq * 32 : (pq + 1) * 32]
    late[:, 0:128] = weight
    late[:, 128:256] = jnp.concatenate([own, jnp.zeros((32, 96), F32)], axis=1)
    late_copy = send(late, late_pair, late_pair_sem, sibling)

    await_bytes(got, rs_sem.at[1])

    def add(k, total):
        return total + got[rows(k), :].astype(F32)

    total = lax.fori_loop(0, 63, add, half[rows(me), :].astype(F32), unroll=9)
    out_ref[rows(me), mine] = total.astype(BF16)

    def gather(k, carry):
        piece = out_ref.at[rows(me), mine]
        copy = pltpu.make_async_remote_copy(
            src_ref=piece, dst_ref=piece, send_sem=gather_send, recv_sem=gather_recv.at[k // 16],
            device_id=(shifted(me, k), core), device_id_type=MESH,
        )
        copy.start()
        return carry

    lax.fori_loop(1, 64, gather, 0)

    late_copy.wait()
    late_sum[...] = late[...] + late_pair[...]

    def along_x(k, carry):
        send(late_sum, late_x.at[k - 1], x_sem, (shifted(me, k), core))
        return carry

    lax.fori_loop(1, 4, along_x, 0)
    await_bytes(late_x, x_sem.at[0])
    await_bytes(late_x, x_sem.at[1])
    late_total[...] = late_sum[...] + (late_x[0] + late_x[1] + late_x[2])

    def across(k, carry):
        send(late_total, late_yz.at[k - 1], yz_sem, (shifted(me, 4 * k), core))
        return carry

    lax.fori_loop(1, 16, across, 0)

    backs = []
    for k in range(4):
        count = 240 if k == 0 else 256
        await_bytes(half.at[0:count, :], gather_recv.at[k])
        block = pl.ds(pl.multiple_of(lax.rem(me // 16 + 4 - k, 4) * 256, 256), 256)
        backs.append(send(out_ref.at[block, mine], out_ref.at[block, mine], back_sem.at[k], sibling))
    await_bytes(late_yz, yz_sem.at[0])
    await_bytes(late_yz, yz_sem.at[1])
    late_out_ref[...] = lax.fori_loop(0, 15, lambda k, total: total + late_yz[k], late_total[...], unroll=5)
    await_bytes(got, rs_sem.at[0])
    await_bytes(got, gather_send)
    for sem in (feat_sem.at[0], feat_sem.at[1]):
        await_bytes(feat_out_ref.at[0:504, :], sem)
    for copy in backs:
        copy.wait()


def unpack_kernel(
    sums_ref, late_ref, feat_ref,
    features_ref, in_one_ref, in_two_ref, out_one_ref, out_two_ref, w_one_ref, w_two_ref,
):
    for i in range(7):
        rows = min(128, 864 - i * 128)
        for k in range(4):
            j = (i + k) % 7
            cols = min(128, 864 - j * 128)
            block = sums_ref[i * 128 : (i + 1) * 128, k * 128 : (k + 1) * 128].astype(F32)
            in_two_ref[i * 128 : i * 128 + rows, j * 128 : j * 128 + cols] = block[0:rows, 0:cols]
            if k:
                in_two_ref[j * 128 : j * 128 + cols, i * 128 : i * 128 + rows] = block.T[0:cols, 0:rows]
    w_two_ref[:, 0:512] = sums_ref[896:960, :].astype(F32)
    rest = sums_ref[960:1024, :].astype(F32)
    w_two_ref[:, 512:864] = rest[:, 0:352]
    out_two_ref[...] = rest[:, 384:448]
    first = sums_ref[864:896, :].astype(F32)
    for k in range(4):
        rows = min(32, 108 - k * 32)
        in_one_ref[k * 32 : k * 32 + rows, :] = first[0:rows, k * 128 : k * 128 + 108]
    late = late_ref[...]
    w_one_ref[...] = late[:, 0:108]
    out_one_ref[...] = late[:, 128:160]
    for r in range(8):
        block = feat_ref[pl.ds(r, 64, stride=8), :]
        features_ref[r * 8 : (r + 1) * 8, 0, :, :] = block.T.reshape(8, 16, 64).astype(BF16)


def local(volume, kernel_one, kernel_two, cotangent):
    shape = jax.ShapeDtypeStruct
    dma = pltpu.SemaphoreType.DMA
    buf = pltpu.VMEM
    sums, late, feat = pl.pallas_call(
        step_kernel,
        name="step",
        out_shape=(shape((1024, 512), BF16), shape((32, 256), F32), shape((512, 128), F32)),
        in_specs=[VM] * 5,
        out_specs=(VM,) * 3,
        scratch_shapes=[
            buf((16, 136, 128), F32), buf((640, 512), F32), buf((4096, 128), F32), buf((640, 1024), BF16),
            buf((512, 640), BF16), buf((128, 1536), BF16), buf((32, 128), BF16), buf((128, 384), BF16),
            buf((256, 1024), F32), buf((128, 1024), BF16), buf((8, 864, 128), F32), buf((1280, 1024), BF16),
            buf((32, 512), F32), buf((1024, 512), BF16), buf((512, 128), F32), buf((64, 1024), BF16),
            buf((864, 128), F32), buf((3, 128, 256), BF16), buf((2, 256, 1024), BF16),
            buf((4, 128, 128), BF16), buf((128, 1024), BF16), buf((64, 1024), BF16),
            buf((1024, 256), BF16), buf((1024, 256), BF16), buf((1008, 256), BF16),
            buf((32, 256), F32), buf((32, 256), F32), buf((3, 32, 256), F32), buf((32, 256), F32),
            buf((15, 32, 256), F32), buf((32, 256), F32),
            dma((2,)), dma((2,)), dma((2,)), dma((8, 2)), dma((2,)), dma((2,)), dma((2,)), dma((2,)), dma((2,)),
            dma, dma((4,)), dma((4, 2)),
        ],
        compiler_params=pltpu.CompilerParams(
            vmem_limit_bytes=VMEM_CAP, collective_id=0, has_side_effects=True
        ),
    )(volume, kernel_one.T, kernel_two.T, cotangent.reshape(64, 1024), tap_matrix())
    features, in_one, in_two, out_one, out_two, w_one, w_two = pl.pallas_call(
        unpack_kernel,
        name="unpack",
        out_shape=(
            shape((64, 1, 16, 64), BF16), shape((108, 108), F32), shape((864, 864), F32), shape((32, 32), F32),
            shape((64, 64), F32), shape((32, 108), F32), shape((64, 864), F32),
        ),
        in_specs=[VM] * 3,
        out_specs=(VM,) * 7,
        compiler_params=pltpu.CompilerParams(vmem_limit_bytes=VMEM_CAP),
    )(sums, late, feat)
    return features.transpose(0, 1, 3, 2), in_one, in_two, out_one, out_two, w_one.T, w_two.T


def solution(mesh):
    placed = (P(None, "batch", "space", None, None), P(), P(), P(None, "batch", "space", None))
    return jax.shard_map(
        local,
        mesh=mesh,
        in_specs=placed,
        out_specs=(P(None, "batch", None, "space"), P(), P(), P(), P(), P(), P()),
        check_vma=False,
    )
```

time: 154 us -> 64 us (0.42)
  the two profiles are of different devices: /device:TPU:1 before, /device:TPU:4 now
where the time goes in v2:
time: 64 us; the launch traced here: 63.8 us
  Pallas kernels  63.2 us (99%)
  between operations  0.64 us (1%)
    pallas_call x1, Pallas kernels, local(): pl.pallas_call(step_kernel, name='step', out_shape=(shape((1024, 512), BF...  59.8 us
    pallas_call x1, Pallas kernels, local(): pl.pallas_call(unpack_kernel, name='unpack', out_shape=(shape((64, 1, 16,...  3.44 us

profile of v2, /device:TPU:4, one launch (start us, length us, event | category | flops | bytes accessed | tf_op | source)
XLA Modules:
  0.0 63.8 jit_solution(13643157971498702084)
XLA Ops:
  0.6 59.8 %step.1 = (bf16[1024,512]{1,0:T(8,128)(2,1)}, f32[32,256]{1,0:T(8,128)}, f32[512,128]{1,0:T(8,128)}) custom-call(bf16[4,1,4,128,128]{4,3,2,1,0:T(8,128)(2,1)} %vol_ref.1, bf16[32,108]{1,0:T(8,128)(2,1)} %bitcast.8, bf16[64,864]{1,0:T(8,128)(2,1)} %bitcast.7, bf16[64,1024]{1,0:T(8,128)(2,1)} %bitcast.6, f32[128,1536]{1,0:T(8,128)} %constant.2.clone.tap_ref), custom_call_target="tpu_custom_call" | custom-call | tf_op jit(solution)/shard_map/step/pallas_call | solution.py:395
  60.4 3.4 %unpack.1 = (bf16[64,1,16,64]{3,2,1,0:T(8,128)(2,1)}, f32[108,108]{1,0:T(8,128)}, f32[864,864]{1,0:T(8,128)}, f32[32,32]{1,0:T(8,128)}, f32[64,64]{1,0:T(8,128)}, /*index=5*/f32[32,108]{1,0:T(8,128)}, f32[64,864]{1,0:T(8,128)}) custom-call(bf16[1024,512]{1,0:T(8,128)(2,1)} %get-tuple-element.17.sums_ref, f32[32,256]{1,0:T(8,128)} %get-tuple-element.18.late_ref, ...), custom_call_target="tpu_custom_call" | custom-call | tf_op jit(solution)/shard_map/unpack/pallas_call | solution.py:418

commit v3 on v2

--- a/solution.py
+++ b/solution.py
@@ -16,16 +16,13 @@
 
 
 def tap_matrix():
-    table = np.zeros((128, 4, 3, 128), np.float32)
-    for p in range(2):
-        for q in range(2):
-            for c in range(4):
-                for a in range(3):
-                    for b in range(3):
-                        for e in range(3):
-                            row = c * 27 + a * 9 + b * 3 + e
-                            table[row, p * 2 + q, a, (2 * q + e) * 20 + c * 5 + 2 * p + b] = 1
-    return jnp.asarray(table.reshape(128, 1536), F32)
+    table = np.zeros((128, 3, 128), np.float32)
+    for c in range(4):
+        for a in range(3):
+            for b in range(3):
+                for e in range(3):
+                    table[c * 27 + a * 9 + b * 3 + e, a, e * 20 + c * 5 + b] = 1
+    return jnp.asarray(table.reshape(128, 384), F32)
 
 
 def gelu_parts(value):
@@ -54,10 +51,7 @@
 
 
 def shifted(me, k):
-    y = lax.rem(me // 16 + k // 16, 4)
-    z = lax.rem(lax.rem(me // 4, 4) + lax.rem(k // 4, 4), 4)
-    x = lax.rem(lax.rem(me, 4) + lax.rem(k, 4), 4)
-    return y * 16 + z * 4 + x
+    return (((me & 48) + (k & 48)) & 48) | (((me & 12) + (k & 12)) & 12) | (((me & 3) + (k & 3)) & 3)
 
 
 def rows(index, count=16):
@@ -166,11 +160,11 @@
 
 
 def step_kernel(
-    vol_ref, k1_ref, k2_ref, cot_ref, tap_ref, out_ref, late_out_ref, feat_out_ref,
-    vf, lf, of, uu, ee, taps, k1p, ww, slopes, hid, p2f, p2b, tiles, sums, feat, g2, k2f, aa, gs,
+    vol_hbm, k1_hbm, k2_hbm, cot_hbm, tap_hbm, out_ref, late_out_ref, feat_out_ref,
+    vol_ref, k1_ref, k2_ref, cot_ref, tap_ref, load_sem, vf, lf, of, uu, ee, taps, k1p, ww, slopes, hid, p2f, p2b, tiles, sums, feat, g2, k2f, aa, gs,
     rim, hid_in, g2_in, pair, half, got, late, late_pair, late_x, late_sum, late_yz, late_total,
     rim_sem, hid_sem, g2_sem, pair_sem, late_pair_sem, rs_sem, feat_sem, x_sem, yz_sem,
-    gather_send, gather_recv, back_sem,
+    gather_send, gather_recv, back_sem, late_back_sem,
 ):
     me, core = lax.axis_index("space"), lax.axis_index("batch")
     sibling = (me, 1 - core)
@@ -188,11 +182,16 @@
     barrier = pltpu.get_barrier_semaphore()
     pl.semaphore_signal(barrier, inc=1, device_id=sibling, device_id_type=MESH)
 
-    def greet(k, carry):
+    for k in range(1, 64):
         pl.semaphore_signal(barrier, inc=1, device_id=(shifted(me, k), core), device_id_type=MESH)
-        return carry
-
-    lax.fori_loop(1, 64, greet, 0)
+    loads = [
+        pltpu.make_async_copy(src, dst, load_sem.at[n])
+        for n, (src, dst) in enumerate(
+            ((vol_hbm, vol_ref), (tap_hbm, tap_ref), (k1_hbm, k1_ref), (k2_hbm, k2_ref), (cot_hbm, cot_ref))
+        )
+    ]
+    for load in loads:
+        load.start()
 
     at_x = lax.broadcasted_iota(jnp.int32, (128, 128), 0)
     lane = lax.broadcasted_iota(jnp.int32, (128, 128), 1)
@@ -203,7 +202,11 @@
     vf[:, 0:8, :] = jnp.zeros((16, 8, 128), F32)
     for zz in range(4):
         of[zz * 1024 + 800 : zz * 1024 + 896, :] = jnp.zeros((96, 128), F32)
-    taps[...] = tap_ref[...].astype(BF16)
+    for load in loads:
+        load.wait()
+    for pq, step in enumerate((0, 40, 2, 42)):
+        moved = tap_ref[...] if step == 0 else pltpu.roll(tap_ref[...], step, 1)
+        taps[:, pq * 384 : (pq + 1) * 384] = moved.astype(BF16)
     k1p[...] = jnp.zeros((32, 128), BF16)
     k1p[:, 0:108] = k1_ref[...]
     wide = dot(k1p[...], taps[...])
@@ -235,16 +238,40 @@
         p2b[0:864, j * 128 : (j + 1) * 128] = p2f[j].astype(BF16)
     p2b[864:896, :] = jnp.zeros((32, 1024), BF16)
     p2b[896:1280, :] = p2b[0:384, :]
+
+    pairs = {}
+
+    def swap_block(i):
+        block = slice(i * 128, (i + 1) * 128)
+        pairs[i] = send(sums.at[block, other], pair.at[block, :], pair_sem.at[i], sibling)
+
+    def add_block(i):
+        block = slice(i * 128, (i + 1) * 128)
+        pairs[i].wait()
+        half[block, :] = (sums[block, mine].astype(F32) + pair[block, :].astype(F32)).astype(BF16)
+
+    def scatter(k):
+        to = shifted(me, k)
+        send(half.at[rows(to), :], got.at[rows(k - 1), :], rs_sem, (to, core))
+
+    for i in (6, 0, 1, 2, 3, 4, 5):
+        block = dot_nt(p2b[i * 128 : (i + 1) * 128, :], p2b[i * 128 : i * 128 + 512, :]) * (1.0 / TOTAL_TWO)
+        sums[i * 128 : (i + 1) * 128, :] = block.astype(BF16)
+        if i == 6:
+            sums[864:896, :] = tiles[...].astype(BF16)
+        swap_block(i)
     act, slope = gelu_parts(dot(k2_ref[...], p2b[0:864, :]))
     g2[...] = (cot_ref[...].astype(F32) * (1.0 / math.sqrt(TOTAL_TWO)) * slope).astype(BF16)
     g2_copy = send(g2, g2_in, g2_sem, below)
     pre_act = act.astype(BF16).astype(F32)
-
-    pairs = []
-
-    def swap_block(i):
-        block = slice(i * 128, (i + 1) * 128)
-        pairs.append(send(sums.at[block, other], pair.at[block, :], pair_sem.at[i], sibling))
+    for i in (6, 0, 1, 2, 3, 4, 5):
+        add_block(i)
+
+    @pl.loop(1, 64)
+    def _(k):
+        @pl.when(shifted(me, k) < 56)
+        def _():
+            scatter(k)
 
     grads = dot_nt(g2[...], p2b[0:896, :])
     own = dot_nt(g2[...], g2[...])
@@ -252,23 +279,14 @@
     sums[960:1024, 0:384] = grads[:, 512:896].astype(BF16)
     sums[960:1024, 384:512] = jnp.concatenate([own, jnp.zeros((64, 64), F32)], axis=1).astype(BF16)
     swap_block(7)
-    for i in (6, 0, 1, 2, 3, 4, 5):
-        block = dot_nt(p2b[i * 128 : (i + 1) * 128, :], p2b[i * 128 : i * 128 + 512, :]) * (1.0 / TOTAL_TWO)
-        sums[i * 128 : (i + 1) * 128, :] = block.astype(BF16)
-        if i == 6:
-            sums[864:896, :] = tiles[...].astype(BF16)
-        swap_block(i)
-    for n, i in enumerate((7, 6, 0, 1, 2, 3, 4, 5)):
-        block = slice(i * 128, (i + 1) * 128)
-        pairs[n].wait()
-        half[block, :] = (sums[block, mine].astype(F32) + pair[block, :].astype(F32)).astype(BF16)
-
-    def scatter(k, carry):
-        to = shifted(me, k)
-        send(half.at[rows(to), :], got.at[rows(k - 1), :], rs_sem, (to, core))
-        return carry
-
-    lax.fori_loop(1, 64, scatter, 0)
+    shift_back(g2[...].astype(F32), gs, 0)
+    add_block(7)
+
+    @pl.loop(1, 64)
+    def _(k):
+        @pl.when(shifted(me, k) >= 56)
+        def _():
+            scatter(k)
 
     moved = swap_groups(pre_act)
     for r in range(8):
@@ -283,7 +301,6 @@
     lax.fori_loop(1, 64, hand_on, 0)
     feat_out_ref[rows(me, 8), :] = feat[rows(me, 8), :]
 
-    shift_back(g2[...].astype(F32), gs, 0)
     g2_copy.wait()
     shift_back(jnp.where(me < 63, g2_in[...].astype(F32), 0.0), gs, 1)
     cross = jnp.zeros((128, 384), F32)
@@ -301,17 +318,24 @@
         for part in halves(cross[pq * 32 : (pq + 1) * 32, :]):
             weight = weight + dot_nt(part, taps[:, pq * 384 : (pq + 1) * 384])
         own = own + gram[pq * 32 : (pq + 1) * 32, pq * 32 : (pq + 1) * 32]
-    late[:, 0:128] = weight
-    late[:, 128:256] = jnp.concatenate([own, jnp.zeros((32, 96), F32)], axis=1)
-    late_copy = send(late, late_pair, late_pair_sem, sibling)
+    late[:, 0:128] = weight.astype(BF16)
+    late[:, 128:256] = jnp.concatenate([own, jnp.zeros((32, 96), F32)], axis=1).astype(BF16)
+    send(late.at[rows(1 - core), :], late_pair, late_pair_sem, sibling).wait()
+    late_sum[...] = (late[rows(core), :].astype(F32) + late_pair[...].astype(F32)).astype(BF16)
+    for k in range(1, 4):
+        send(late_sum, late_x.at[k - 1], x_sem, (shifted(me, k), core))
+    await_bytes(late_x, x_sem.at[0])
+    await_bytes(late_x, x_sem.at[1])
+    near = late_sum[...].astype(F32) + late_x[0].astype(F32) + (late_x[1].astype(F32) + late_x[2].astype(F32))
+    late_total[...] = near.astype(BF16)
+    for k in range(1, 16):
+        send(late_total, late_yz.at[k - 1], yz_sem, (shifted(me, 4 * k), core))
 
     await_bytes(got, rs_sem.at[1])
-
-    def add(k, total):
-        return total + got[rows(k), :].astype(F32)
-
-    total = lax.fori_loop(0, 63, add, half[rows(me), :].astype(F32), unroll=9)
-    out_ref[rows(me), mine] = total.astype(BF16)
+    parts = [half[rows(me), :].astype(F32), jnp.zeros((16, 256), F32)]
+    for k in range(63):
+        parts[k % 2] = parts[k % 2] + got[k * 16 : (k + 1) * 16, :].astype(F32)
+    out_ref[rows(me), mine] = (parts[0] + parts[1]).astype(BF16)
 
     def gather(k, carry):
         piece = out_ref.at[rows(me), mine]
@@ -324,24 +348,6 @@
 
     lax.fori_loop(1, 64, gather, 0)
 
-    late_copy.wait()
-    late_sum[...] = late[...] + late_pair[...]
-
-    def along_x(k, carry):
-        send(late_sum, late_x.at[k - 1], x_sem, (shifted(me, k), core))
-        return carry
-
-    lax.fori_loop(1, 4, along_x, 0)
-    await_bytes(late_x, x_sem.at[0])
-    await_bytes(late_x, x_sem.at[1])
-    late_total[...] = late_sum[...] + (late_x[0] + late_x[1] + late_x[2])
-
-    def across(k, carry):
-        send(late_total, late_yz.at[k - 1], yz_sem, (shifted(me, 4 * k), core))
-        return carry
-
-    lax.fori_loop(1, 16, across, 0)
-
     backs = []
     for k in range(4):
         count = 240 if k == 0 else 256
@@ -350,7 +356,11 @@
         backs.append(send(out_ref.at[block, mine], out_ref.at[block, mine], back_sem.at[k], sibling))
     await_bytes(late_yz, yz_sem.at[0])
     await_bytes(late_yz, yz_sem.at[1])
-    late_out_ref[...] = lax.fori_loop(0, 15, lambda k, total: total + late_yz[k], late_total[...], unroll=5)
+    far = late_total[...].astype(F32)
+    for k in range(15):
+        far = far + late_yz[k].astype(F32)
+    late_out_ref[rows(core), :] = far
+    backs.append(send(late_out_ref.at[rows(core), :], late_out_ref.at[rows(core), :], late_back_sem, sibling))
     await_bytes(got, rs_sem.at[0])
     await_bytes(got, gather_send)
     for sem in (feat_sem.at[0], feat_sem.at[1]):
@@ -361,31 +371,38 @@
 
 def unpack_kernel(
     sums_ref, late_ref, feat_ref,
-    features_ref, in_one_ref, in_two_ref, out_one_ref, out_two_ref, w_one_ref, w_two_ref,
+    features_ref, in_one_ref, in_two_hbm, out_one_ref, out_two_ref, w_one_ref, w_two_ref, in_two, store_sem,
 ):
+    stores = []
     for i in range(7):
-        rows = min(128, 864 - i * 128)
-        for k in range(4):
+        height = min(128, 864 - i * 128)
+        band = slice(i * 128, i * 128 + height)
+        for k in range(-3, 4):
             j = (i + k) % 7
-            cols = min(128, 864 - j * 128)
-            block = sums_ref[i * 128 : (i + 1) * 128, k * 128 : (k + 1) * 128].astype(F32)
-            in_two_ref[i * 128 : i * 128 + rows, j * 128 : j * 128 + cols] = block[0:rows, 0:cols]
-            if k:
-                in_two_ref[j * 128 : j * 128 + cols, i * 128 : i * 128 + rows] = block.T[0:cols, 0:rows]
+            width = min(128, 864 - j * 128)
+            if k >= 0:
+                block = sums_ref[i * 128 : (i + 1) * 128, k * 128 : (k + 1) * 128].astype(F32)
+            else:
+                block = sums_ref[j * 128 : (j + 1) * 128, -k * 128 : (1 - k) * 128].astype(F32).T
+            in_two[band, j * 128 : j * 128 + width] = block[0:height, 0:width]
+        stores.append(pltpu.make_async_copy(in_two.at[band, :], in_two_hbm.at[band, :], store_sem.at[i]))
+        stores[-1].start()
     w_two_ref[:, 0:512] = sums_ref[896:960, :].astype(F32)
     rest = sums_ref[960:1024, :].astype(F32)
     w_two_ref[:, 512:864] = rest[:, 0:352]
     out_two_ref[...] = rest[:, 384:448]
     first = sums_ref[864:896, :].astype(F32)
     for k in range(4):
-        rows = min(32, 108 - k * 32)
-        in_one_ref[k * 32 : k * 32 + rows, :] = first[0:rows, k * 128 : k * 128 + 108]
+        height = min(32, 108 - k * 32)
+        in_one_ref[k * 32 : k * 32 + height, :] = first[0:height, k * 128 : k * 128 + 108]
     late = late_ref[...]
     w_one_ref[...] = late[:, 0:108]
     out_one_ref[...] = late[:, 128:160]
     for r in range(8):
         block = feat_ref[pl.ds(r, 64, stride=8), :]
         features_ref[r * 8 : (r + 1) * 8, 0, :, :] = block.T.reshape(8, 16, 64).astype(BF16)
+    for store in stores:
+        store.wait()
 
 
 def local(volume, kernel_one, kernel_two, cotangent):
@@ -396,9 +413,11 @@
         step_kernel,
         name="step",
         out_shape=(shape((1024, 512), BF16), shape((32, 256), F32), shape((512, 128), F32)),
-        in_specs=[VM] * 5,
+        in_specs=[pl.BlockSpec(memory_space=pl.ANY)] * 5,
         out_specs=(VM,) * 3,
         scratch_shapes=[
+            buf((4, 1, 4, 128, 128), BF16), buf((32, 108), BF16), buf((64, 864), BF16), buf((64, 1024), BF16),
+            buf((128, 384), F32), dma((5,)),
             buf((16, 136, 128), F32), buf((640, 512), F32), buf((4096, 128), F32), buf((640, 1024), BF16),
             buf((512, 640), BF16), buf((128, 1536), BF16), buf((32, 128), BF16), buf((128, 384), BF16),
             buf((256, 1024), F32), buf((128, 1024), BF16), buf((8, 864, 128), F32), buf((1280, 1024), BF16),
@@ -406,10 +425,10 @@
             buf((864, 128), F32), buf((3, 128, 256), BF16), buf((2, 256, 1024), BF16),
             buf((4, 128, 128), BF16), buf((128, 1024), BF16), buf((64, 1024), BF16),
             buf((1024, 256), BF16), buf((1024, 256), BF16), buf((1008, 256), BF16),
-            buf((32, 256), F32), buf((32, 256), F32), buf((3, 32, 256), F32), buf((32, 256), F32),
-            buf((15, 32, 256), F32), buf((32, 256), F32),
+            buf((32, 256), BF16), buf((16, 256), BF16), buf((3, 16, 256), BF16), buf((16, 256), BF16),
+            buf((15, 16, 256), BF16), buf((16, 256), BF16),
             dma((2,)), dma((2,)), dma((2,)), dma((8, 2)), dma((2,)), dma((2,)), dma((2,)), dma((2,)), dma((2,)),
-            dma, dma((4,)), dma((4, 2)),
+            dma, dma((4,)), dma((4, 2)), dma((2,)),
         ],
         compiler_params=pltpu.CompilerParams(
             vmem_limit_bytes=VMEM_CAP, collective_id=0, has_side_effects=True
@@ -423,7 +442,8 @@
             shape((64, 64), F32), shape((32, 108), F32), shape((64, 864), F32),
         ),
         in_specs=[VM] * 3,
-        out_specs=(VM,) * 7,
+        out_specs=(VM, VM, pl.BlockSpec(memory_space=pl.ANY), VM, VM, VM, VM),
+        scratch_shapes=[buf((864, 864), F32), dma((7,))],
         compiler_params=pltpu.CompilerParams(vmem_limit_bytes=VMEM_CAP),
     )(sums, late, feat)
     return features.transpose(0, 1, 3, 2), in_one, in_two, out_one, out_two, w_one.T, w_two.T

time: 64 us -> 61.3 us (0.958)
  the two profiles are of different devices: /device:TPU:4 before, /device:TPU:1 now
where the time goes in v3:
time: 61.3 us; the launch traced here: 61.1 us
  Pallas kernels  60.5 us (99%)
  between operations  0.64 us (1%)
    pallas_call x1, Pallas kernels, local(): pl.pallas_call(step_kernel, name='step', out_shape=(shape((1024, 512), BF...  56.6 us
    pallas_call x1, Pallas kernels, local(): pl.pallas_call(unpack_kernel, name='unpack', out_shape=(shape((64, 1, 16,...  3.91 us

profile of v3, /device:TPU:1, one launch (start us, length us, event | category | flops | bytes accessed | tf_op | source)
XLA Modules:
  0.0 61.1 jit_solution(8844043696839583585)
XLA Ops:
  0.6 56.6 %step.1 = (bf16[1024,512]{1,0:T(8,128)(2,1)}, f32[32,256]{1,0:T(8,128)}, f32[512,128]{1,0:T(8,128)}) custom-call(bf16[4,1,4,128,128]{4,3,2,1,0:T(8,128)(2,1)} %vol_hbm.1, bf16[32,108]{1,0:T(8,128)(2,1)} %bitcast.8, bf16[64,864]{1,0:T(8,128)(2,1)} %bitcast.7, bf16[64,1024]{1,0:T(8,128)(2,1)} %bitcast.6, f32[128,384]{1,0:T(8,128)} %constant.2.clone.tap_hbm), custom_call_target="tpu_custom_call" | custom-call | tf_op jit(solution)/shard_map/step/pallas_call | solution.py:412
  57.2 3.9 %unpack.1 = (bf16[64,1,16,64]{3,2,1,0:T(8,128)(2,1)}, f32[108,108]{1,0:T(8,128)}, f32[864,864]{1,0:T(8,128)}, f32[32,32]{1,0:T(8,128)}, f32[64,64]{1,0:T(8,128)}, /*index=5*/f32[32,108]{1,0:T(8,128)}, f32[64,864]{1,0:T(8,128)}) custom-call(bf16[1024,512]{1,0:T(8,128)(2,1)} %get-tuple-element.17.sums_ref, f32[32,256]{1,0:T(8,128)} %get-tuple-element.18.late_ref, ...), custom_call_target="tpu_custom_call" | custom-call | tf_op jit(solution)/shard_map/unpack/pallas_call | solution.py:437

commit v4 on v3

--- a/solution.py
+++ b/solution.py
@@ -122,16 +122,14 @@
         tiles[:, k * 128 : (k + 1) * 128] = total[k * 32 : (k + 1) * 32, :]
 
 
-def swap_groups(act):
-    chan = lax.broadcasted_iota(jnp.int32, (64, 1024), 0) % 8
-    group = (lax.broadcasted_iota(jnp.int32, (64, 1024), 1) // 16) % 8
-    for bit in (4, 2, 1):
-        down = pltpu.roll(pltpu.roll(act, 64 - bit, 0), bit * 16, 1)
-        up = pltpu.roll(pltpu.roll(act, bit, 0), 1024 - bit * 16, 1)
-        in_chan = (chan & bit) != 0
-        in_group = (group & bit) != 0
-        act = jnp.where(in_chan == in_group, act, jnp.where(in_group, down, up))
-    return act
+def group_matrix(half_tile, pick):
+    lane = lax.broadcasted_iota(jnp.int32, (128, 128), 0) - half_tile * 64
+    col = lax.broadcasted_iota(jnp.int32, (128, 128), 1)
+    for low in range(8):
+        inside = (col >= low * 16) & (col < (low + 1) * 16)
+        for x in range(4):
+            hit = inside & (lane == x * 16 + col - low * 16)
+            pick[low * 128 : (low + 1) * 128, x * 128 : (x + 1) * 128] = jnp.where(hit, 1.0, 0.0).astype(BF16)
 
 
 def backward_weights(k2_ref, k2f, aa):
@@ -147,6 +145,14 @@
                 aa[a, at : at + 32, (sy * 2 + sx) * 64 : (sy * 2 + sx + 1) * 64] = block[:, 0:64].astype(BF16)
 
 
+def layer_two_part(aa, a, plane):
+    lane = lax.broadcasted_iota(jnp.int32, (1, 1024), 1)
+    parts = lax.dot_general(aa[a], plane, (((0,), (0,)), ((), ())), preferred_element_type=F32)
+    low = parts[0:64] + jnp.where(lane % 32 == 0, 0.0, pltpu.roll(parts[64:128], 1, 1))
+    high = parts[128:192] + jnp.where(lane % 32 == 0, 0.0, pltpu.roll(parts[192:256], 1, 1))
+    return low + jnp.where(lane < 32, 0.0, pltpu.roll(high, 32, 1))
+
+
 def shift_back(value, gs, n):
     lane = lax.broadcasted_iota(jnp.int32, (1, 1024), 1)
     for sy in range(2):
@@ -161,9 +167,9 @@
 
 def step_kernel(
     vol_hbm, k1_hbm, k2_hbm, cot_hbm, tap_hbm, out_ref, late_out_ref, feat_out_ref,
-    vol_ref, k1_ref, k2_ref, cot_ref, tap_ref, load_sem, vf, lf, of, uu, ee, taps, k1p, ww, slopes, hid, p2f, p2b, tiles, sums, feat, g2, k2f, aa, gs,
+    vol_ref, k1_ref, k2_ref, cot_ref, tap_ref, load_sem, vf, lf, of, uu, ee, taps, k1p, ww, slopes, hid, pre_two, p2f, p2b, tiles, sums, feat, feat_near, feat_mid, feat_far, pick, g2, k2f, aa, gs,
     rim, hid_in, g2_in, pair, half, got, late, late_pair, late_x, late_sum, late_yz, late_total,
-    rim_sem, hid_sem, g2_sem, pair_sem, late_pair_sem, rs_sem, feat_sem, x_sem, yz_sem,
+    rim_sem, hid_sem, g2_sem, pair_sem, late_pair_sem, rs_sem, feat_sem, far_sem, x_sem, yz_sem,
     gather_send, gather_recv, back_sem, late_back_sem,
 ):
     me, core = lax.axis_index("space"), lax.axis_index("batch")
@@ -213,15 +219,19 @@
     for pq in range(4):
         ww[pq * 32 : (pq + 1) * 32, :] = wide[:, pq * 384 : (pq + 1) * 384].astype(BF16)
 
-    spread_planes(1, 4, lambda c, zz: vol_ref[c, 0, zz].astype(F32), vf, lf, of, uu, ee)
     pl.semaphore_wait(barrier, 64)
     rim_copy = send(vol_ref.at[:, 0, 3], rim, rim_sem, above)
+
+    spread_planes(1, 4, lambda c, zz: vol_ref[c, 0, zz].astype(F32), vf, lf, of, uu, ee)
     act, slope = gelu_parts(dot(ww[...], uu[256:640, :]))
     slopes[128:256, :] = slope
     hid[...] = act.astype(BF16)
     hid_copy = send(hid, hid_in, hid_sem, above)
     place_taps(hid[...].astype(F32), 2, p2f)
     backward_weights(k2_ref, k2f, aa)
+    pre_two[...] = layer_two_part(aa, 2, hid[...])
+
+    group_matrix((me // 4) & 1, pick)
 
     rim_copy.wait()
     spread_planes(
@@ -229,78 +239,75 @@
     )
     act, slope = gelu_parts(dot(ww[...], uu[0:384, :]))
     slopes[0:128, :] = slope
-    place_taps(act.astype(BF16).astype(F32), 1, p2f)
+    act = act.astype(BF16)
+    place_taps(act.astype(F32), 1, p2f)
+    pre_two[...] += layer_two_part(aa, 1, act)
     first_factor(uu, taps, tiles)
 
     hid_copy.wait()
-    place_taps(jnp.where(me > 0, hid_in[...].astype(F32), 0.0), 0, p2f)
+    lower = jnp.where(me > 0, hid_in[...].astype(F32), 0.0)
+    act, slope = gelu_parts(pre_two[...] + layer_two_part(aa, 0, lower.astype(BF16)))
+    g2[...] = (cot_ref[...].astype(F32) * (1.0 / math.sqrt(TOTAL_TWO)) * slope).astype(BF16)
+    g2_copy = send(g2, g2_in, g2_sem, below)
+
+    feat[...] = act.astype(BF16)
+    plane = me // 4
+    half_tile = plane & 1
+
+    @pl.loop(1, 16)
+    def _(k):
+        to = shifted(me, 4 * k)
+        tile = pl.ds(pl.multiple_of((to // 8) * 128, 128), 128)
+        send(feat.at[:, tile], feat_near.at[plane], feat_sem, (to, core))
+
+    feat_near[plane] = feat[:, pl.ds(pl.multiple_of((me // 8) * 128, 128), 128)]
+
+    place_taps(lower, 0, p2f)
     for j in range(8):
         p2b[0:864, j * 128 : (j + 1) * 128] = p2f[j].astype(BF16)
     p2b[864:896, :] = jnp.zeros((32, 1024), BF16)
     p2b[896:1280, :] = p2b[0:384, :]
 
-    pairs = {}
-
-    def swap_block(i):
-        block = slice(i * 128, (i + 1) * 128)
-        pairs[i] = send(sums.at[block, other], pair.at[block, :], pair_sem.at[i], sibling)
-
-    def add_block(i):
-        block = slice(i * 128, (i + 1) * 128)
-        pairs[i].wait()
-        half[block, :] = (sums[block, mine].astype(F32) + pair[block, :].astype(F32)).astype(BF16)
-
-    def scatter(k):
-        to = shifted(me, k)
-        send(half.at[rows(to), :], got.at[rows(k - 1), :], rs_sem, (to, core))
-
-    for i in (6, 0, 1, 2, 3, 4, 5):
-        block = dot_nt(p2b[i * 128 : (i + 1) * 128, :], p2b[i * 128 : i * 128 + 512, :]) * (1.0 / TOTAL_TWO)
-        sums[i * 128 : (i + 1) * 128, :] = block.astype(BF16)
-        if i == 6:
-            sums[864:896, :] = tiles[...].astype(BF16)
-        swap_block(i)
-    act, slope = gelu_parts(dot(k2_ref[...], p2b[0:864, :]))
-    g2[...] = (cot_ref[...].astype(F32) * (1.0 / math.sqrt(TOTAL_TWO)) * slope).astype(BF16)
-    g2_copy = send(g2, g2_in, g2_sem, below)
-    pre_act = act.astype(BF16).astype(F32)
-    for i in (6, 0, 1, 2, 3, 4, 5):
-        add_block(i)
-
-    @pl.loop(1, 64)
-    def _(k):
-        @pl.when(shifted(me, k) < 56)
-        def _():
-            scatter(k)
+    def gram_part(side):
+        lanes = pl.ds(pl.multiple_of(side * 256, 256), 256)
+        for i in range(7):
+            cols = pl.ds(pl.multiple_of(i * 128 + side * 256, 128), 256)
+            block = dot_nt(p2b[i * 128 : (i + 1) * 128, :], p2b[cols, :]) * (1.0 / TOTAL_TWO)
+            sums[i * 128 : (i + 1) * 128, lanes] = block.astype(BF16)
+        sums[864:896, lanes] = tiles[:, lanes].astype(BF16)
 
     grads = dot_nt(g2[...], p2b[0:896, :])
     own = dot_nt(g2[...], g2[...])
     sums[896:960, :] = grads[:, 0:512].astype(BF16)
     sums[960:1024, 0:384] = grads[:, 512:896].astype(BF16)
     sums[960:1024, 384:512] = jnp.concatenate([own, jnp.zeros((64, 64), F32)], axis=1).astype(BF16)
-    swap_block(7)
+    gram_part(1 - core)
+    pair_copy = send(sums.at[:, other], pair, pair_sem, sibling)
+    gram_part(core)
+    pair_copy.wait()
+    half[...] = (sums[:, mine].astype(F32) + pair[...].astype(F32)).astype(BF16)
+
+    def scatter(k, carry):
+        to = shifted(me, k)
+        send(half.at[rows(to), :], got.at[rows(k - 1), :], rs_sem, (to, core))
+        return carry
+
+    lax.fori_loop(1, 64, scatter, 0)
+
+    for sem in (feat_sem.at[0], feat_sem.at[1]):
+        await_bytes(feat_near.at[0:15], sem)
+    for k in range(16):
+        feat_mid[k * 64 : (k + 1) * 64, :] = feat_near[k].astype(F32)
+    wide = jnp.concatenate([feat_mid[pl.ds(low, 128, stride=8), :] for low in range(8)], axis=1).astype(BF16)
+    wide = dot(wide, pick[...]).astype(BF16)
+    for x in range(4):
+        feat_far[x] = wide[:, x * 128 : (x + 1) * 128]
+    for k in range(1, 4):
+        to = shifted(me, k)
+        send(feat_far.at[to & 3], feat_out_ref.at[me & 3], far_sem, (to, core))
+    feat_out_ref[me & 3] = feat_far[me & 3]
+
     shift_back(g2[...].astype(F32), gs, 0)
-    add_block(7)
-
-    @pl.loop(1, 64)
-    def _(k):
-        @pl.when(shifted(me, k) >= 56)
-        def _():
-            scatter(k)
-
-    moved = swap_groups(pre_act)
-    for r in range(8):
-        for g in range(8):
-            feat[pl.ds(64 * g + r, 8, stride=8), :] = moved[r * 8 : (r + 1) * 8, g * 128 : (g + 1) * 128]
-
-    def hand_on(k, carry):
-        to = shifted(me, k)
-        send(feat.at[rows(to, 8), :], feat_out_ref.at[rows(me, 8), :], feat_sem, (to, core))
-        return carry
-
-    lax.fori_loop(1, 64, hand_on, 0)
-    feat_out_ref[rows(me, 8), :] = feat[rows(me, 8), :]
-
     g2_copy.wait()
     shift_back(jnp.where(me < 63, g2_in[...].astype(F32), 0.0), gs, 1)
     cross = jnp.zeros((128, 384), F32)
@@ -363,17 +370,19 @@
     backs.append(send(late_out_ref.at[rows(core), :], late_out_ref.at[rows(core), :], late_back_sem, sibling))
     await_bytes(got, rs_sem.at[0])
     await_bytes(got, gather_send)
-    for sem in (feat_sem.at[0], feat_sem.at[1]):
-        await_bytes(feat_out_ref.at[0:504, :], sem)
+    for sem in (far_sem.at[0], far_sem.at[1]):
+        await_bytes(feat_far.at[0:3], sem)
     for copy in backs:
         copy.wait()
 
 
 def unpack_kernel(
     sums_ref, late_ref, feat_ref,
-    features_ref, in_one_ref, in_two_hbm, out_one_ref, out_two_ref, w_one_ref, w_two_ref, in_two, store_sem,
+    features_ref, in_one_ref, in_two_hbm, out_one_ref, out_two_ref, w_one_ref, w_two_ref, in_two, feat, store_sem,
 ):
     stores = []
+    row = lax.broadcasted_iota(jnp.int32, (128, 128), 0)
+    eye = jnp.where(row == lax.broadcasted_iota(jnp.int32, (128, 128), 1), 1.0, 0.0).astype(BF16)
     for i in range(7):
         height = min(128, 864 - i * 128)
         band = slice(i * 128, i * 128 + height)
@@ -383,7 +392,7 @@
             if k >= 0:
                 block = sums_ref[i * 128 : (i + 1) * 128, k * 128 : (k + 1) * 128].astype(F32)
             else:
-                block = sums_ref[j * 128 : (j + 1) * 128, -k * 128 : (1 - k) * 128].astype(F32).T
+                block = dot_nt(eye, sums_ref[j * 128 : (j + 1) * 128, -k * 128 : (1 - k) * 128])
             in_two[band, j * 128 : j * 128 + width] = block[0:height, 0:width]
         stores.append(pltpu.make_async_copy(in_two.at[band, :], in_two_hbm.at[band, :], store_sem.at[i]))
         stores[-1].start()
@@ -398,9 +407,14 @@
     late = late_ref[...]
     w_one_ref[...] = late[:, 0:108]
     out_one_ref[...] = late[:, 128:160]
+    for x in range(4):
+        plane = feat_ref[x].astype(F32)
+        for yz in range(16):
+            at = (yz * 4 + x) * 8
+            feat[at : at + 8, :] = plane[yz * 8 : (yz + 1) * 8, :]
     for r in range(8):
-        block = feat_ref[pl.ds(r, 64, stride=8), :]
-        features_ref[r * 8 : (r + 1) * 8, 0, :, :] = block.T.reshape(8, 16, 64).astype(BF16)
+        block = feat[pl.ds(r, 64, stride=8), :]
+        features_ref[r * 8 : (r + 1) * 8, 0, :, :] = dot_nt(eye, block.astype(BF16)).reshape(8, 16, 64).astype(BF16)
     for store in stores:
         store.wait()
 
@@ -412,7 +426,7 @@
     sums, late, feat = pl.pallas_call(
         step_kernel,
         name="step",
-        out_shape=(shape((1024, 512), BF16), shape((32, 256), F32), shape((512, 128), F32)),
+        out_shape=(shape((1024, 512), BF16), shape((32, 256), F32), shape((4, 128, 128), BF16)),
         in_specs=[pl.BlockSpec(memory_space=pl.ANY)] * 5,
         out_specs=(VM,) * 3,
         scratch_shapes=[
@@ -420,14 +434,15 @@
             buf((128, 384), F32), dma((5,)),
             buf((16, 136, 128), F32), buf((640, 512), F32), buf((4096, 128), F32), buf((640, 1024), BF16),
             buf((512, 640), BF16), buf((128, 1536), BF16), buf((32, 128), BF16), buf((128, 384), BF16),
-            buf((256, 1024), F32), buf((128, 1024), BF16), buf((8, 864, 128), F32), buf((1280, 1024), BF16),
-            buf((32, 512), F32), buf((1024, 512), BF16), buf((512, 128), F32), buf((64, 1024), BF16),
+            buf((256, 1024), F32), buf((128, 1024), BF16), buf((64, 1024), F32), buf((8, 864, 128), F32), buf((1280, 1024), BF16),
+            buf((32, 512), F32), buf((1024, 512), BF16), buf((64, 1024), BF16), buf((16, 64, 128), BF16), buf((1024, 128), F32),
+            buf((4, 128, 128), BF16), buf((1024, 512), BF16), buf((64, 1024), BF16),
             buf((864, 128), F32), buf((3, 128, 256), BF16), buf((2, 256, 1024), BF16),
             buf((4, 128, 128), BF16), buf((128, 1024), BF16), buf((64, 1024), BF16),
             buf((1024, 256), BF16), buf((1024, 256), BF16), buf((1008, 256), BF16),
             buf((32, 256), BF16), buf((16, 256), BF16), buf((3, 16, 256), BF16), buf((16, 256), BF16),
             buf((15, 16, 256), BF16), buf((16, 256), BF16),
-            dma((2,)), dma((2,)), dma((2,)), dma((8, 2)), dma((2,)), dma((2,)), dma((2,)), dma((2,)), dma((2,)),
+            dma((2,)), dma((2,)), dma((2,)), dma((2,)), dma((2,)), dma((2,)), dma((2,)), dma((2,)), dma((2,)), dma((2,)),
             dma, dma((4,)), dma((4, 2)), dma((2,)),
         ],
         compiler_params=pltpu.CompilerParams(
@@ -443,7 +458,7 @@
         ),
         in_specs=[VM] * 3,
         out_specs=(VM, VM, pl.BlockSpec(memory_space=pl.ANY), VM, VM, VM, VM),
-        scratch_shapes=[buf((864, 864), F32), dma((7,))],
+        scratch_shapes=[buf((864, 864), F32), buf((512, 128), F32), dma((7,))],
         compiler_params=pltpu.CompilerParams(vmem_limit_bytes=VMEM_CAP),
     )(sums, late, feat)
     return features.transpose(0, 1, 3, 2), in_one, in_two, out_one, out_two, w_one.T, w_two.T

time: 61.3 us -> 54 us (0.88)
  Pallas kernels: 60.5 us -> 53.2 us
    pallas_call x1, Pallas kernels: 56.6 us -> 49.2 us  [local(): pl.pallas_call(step_kernel, name='step', out_shape=(shape((1024, 512), BF...]
where the time goes in v4:
time: 54 us; the launch traced here: 53.8 us
  Pallas kernels  53.2 us (99%)
  between operations  0.64 us (1%)
    pallas_call x1, Pallas kernels, local(): pl.pallas_call(step_kernel, name='step', out_shape=(shape((1024, 512), BF...  49.2 us
    pallas_call x1, Pallas kernels, local(): pl.pallas_call(unpack_kernel, name='unpack', out_shape=(shape((64, 1, 16,...  4.02 us

profile of v4, /device:TPU:1, one launch (start us, length us, event | category | flops | bytes accessed | tf_op | source)
XLA Modules:
  0.0 53.8 jit_solution(5463926573172831688)
XLA Ops:
  0.6 49.2 %step.1 = (bf16[1024,512]{1,0:T(8,128)(2,1)}, f32[32,256]{1,0:T(8,128)}, bf16[4,128,128]{2,1,0:T(8,128)(2,1)}) custom-call(bf16[4,1,4,128,128]{4,3,2,1,0:T(8,128)(2,1)} %vol_hbm.1, bf16[32,108]{1,0:T(8,128)(2,1)} %bitcast.8, bf16[64,864]{1,0:T(8,128)(2,1)} %bitcast.7, bf16[64,1024]{1,0:T(8,128)(2,1)} %bitcast.6, f32[128,384]{1,0:T(8,128)} %constant.2.clone.tap_hbm), custom_call_target="tpu_custom_call" | custom-call | tf_op jit(solution)/shard_map/step/pallas_call | solution.py:426
  49.8 4.0 %unpack.1 = (bf16[64,1,16,64]{3,2,1,0:T(8,128)(2,1)}, f32[108,108]{1,0:T(8,128)}, f32[864,864]{1,0:T(8,128)}, f32[32,32]{1,0:T(8,128)}, f32[64,64]{1,0:T(8,128)}, /*index=5*/f32[32,108]{1,0:T(8,128)}, f32[64,864]{1,0:T(8,128)}) custom-call(bf16[1024,512]{1,0:T(8,128)(2,1)} %get-tuple-element.17.sums_ref, f32[32,256]{1,0:T(8,128)} %get-tuple-element.18.late_ref, ...), custom_call_target="tpu_custom_call" | custom-call | tf_op jit(solution)/shard_map/unpack/pallas_call | solution.py:452

commit v5 on v4

--- a/solution.py
+++ b/solution.py
@@ -166,11 +166,11 @@
 
 
 def step_kernel(
-    vol_hbm, k1_hbm, k2_hbm, cot_hbm, tap_hbm, out_ref, late_out_ref, feat_out_ref,
+    vol_hbm, k1_hbm, k2_hbm, cot_hbm, tap_hbm, out_hbm, late_hbm, feat_hbm,
     vol_ref, k1_ref, k2_ref, cot_ref, tap_ref, load_sem, vf, lf, of, uu, ee, taps, k1p, ww, slopes, hid, pre_two, p2f, p2b, tiles, sums, feat, feat_near, feat_mid, feat_far, pick, g2, k2f, aa, gs,
-    rim, hid_in, g2_in, pair, half, got, late, late_pair, late_x, late_sum, late_yz, late_total,
-    rim_sem, hid_sem, g2_sem, pair_sem, late_pair_sem, rs_sem, feat_sem, far_sem, x_sem, yz_sem,
-    gather_send, gather_recv, back_sem, late_back_sem,
+    rim, hid_in, g2_in, pair, half, got, piece, late, late_pair, late_x, late_sum, late_yz, late_total, late_far,
+    rim_sem, hid_sem, g2_sem, pair_sem, late_pair_sem, rs_send, rs_recv, feat_sem, far_sem, x_sem, yz_sem,
+    gather_send, gather_recv, back_sem, late_back_sem, keep_sem,
 ):
     me, core = lax.axis_index("space"), lax.axis_index("batch")
     sibling = (me, 1 - core)
@@ -276,23 +276,51 @@
             sums[i * 128 : (i + 1) * 128, lanes] = block.astype(BF16)
         sums[864:896, lanes] = tiles[:, lanes].astype(BF16)
 
+    def swap_rows(n, block):
+        return send(sums.at[block, other], pair.at[block, :], pair_sem.at[n], sibling)
+
+    def add_rows(block):
+        half[block, :] = (sums[block, mine].astype(F32) + pair[block, :].astype(F32)).astype(BF16)
+
+    def scatter(k, to):
+        copy = pltpu.make_async_remote_copy(
+            src_ref=half.at[rows(to), :], dst_ref=got.at[rows(k - 1), :], send_sem=rs_send,
+            recv_sem=rs_recv.at[k // 16], device_id=(to, core), device_id_type=MESH,
+        )
+        copy.start()
+
+    early, late_rows = slice(0, 896), slice(896, 1024)
+    gram_part(1 - core)
+    pair_copy = swap_rows(0, early)
+    gram_part(core)
+    pair_copy.wait()
+    add_rows(early)
+
+    @pl.loop(1, 64)
+    def _(k):
+        to = shifted(me, k)
+
+        @pl.when(to < 56)
+        def _():
+            scatter(k, to)
+
     grads = dot_nt(g2[...], p2b[0:896, :])
     own = dot_nt(g2[...], g2[...])
     sums[896:960, :] = grads[:, 0:512].astype(BF16)
     sums[960:1024, 0:384] = grads[:, 512:896].astype(BF16)
     sums[960:1024, 384:512] = jnp.concatenate([own, jnp.zeros((64, 64), F32)], axis=1).astype(BF16)
-    gram_part(1 - core)
-    pair_copy = send(sums.at[:, other], pair, pair_sem, sibling)
-    gram_part(core)
+    pair_copy = swap_rows(1, late_rows)
+    shift_back(g2[...].astype(F32), gs, 0)
     pair_copy.wait()
-    half[...] = (sums[:, mine].astype(F32) + pair[...].astype(F32)).astype(BF16)
-
-    def scatter(k, carry):
+    add_rows(late_rows)
+
+    @pl.loop(1, 64)
+    def _(k):
         to = shifted(me, k)
-        send(half.at[rows(to), :], got.at[rows(k - 1), :], rs_sem, (to, core))
-        return carry
-
-    lax.fori_loop(1, 64, scatter, 0)
+
+        @pl.when(to >= 56)
+        def _():
+            scatter(k, to)
 
     for sem in (feat_sem.at[0], feat_sem.at[1]):
         await_bytes(feat_near.at[0:15], sem)
@@ -304,10 +332,10 @@
         feat_far[x] = wide[:, x * 128 : (x + 1) * 128]
     for k in range(1, 4):
         to = shifted(me, k)
-        send(feat_far.at[to & 3], feat_out_ref.at[me & 3], far_sem, (to, core))
-    feat_out_ref[me & 3] = feat_far[me & 3]
-
-    shift_back(g2[...].astype(F32), gs, 0)
+        send(feat_far.at[to & 3], feat_hbm.at[me & 3], far_sem, (to, core))
+    feat_keep = pltpu.make_async_copy(feat_far.at[me & 3], feat_hbm.at[me & 3], keep_sem.at[2])
+    feat_keep.start()
+
     g2_copy.wait()
     shift_back(jnp.where(me < 63, g2_in[...].astype(F32), 0.0), gs, 1)
     cross = jnp.zeros((128, 384), F32)
@@ -338,37 +366,44 @@
     for k in range(1, 16):
         send(late_total, late_yz.at[k - 1], yz_sem, (shifted(me, 4 * k), core))
 
-    await_bytes(got, rs_sem.at[1])
     parts = [half[rows(me), :].astype(F32), jnp.zeros((16, 256), F32)]
-    for k in range(63):
-        parts[k % 2] = parts[k % 2] + got[k * 16 : (k + 1) * 16, :].astype(F32)
-    out_ref[rows(me), mine] = (parts[0] + parts[1]).astype(BF16)
-
-    def gather(k, carry):
-        piece = out_ref.at[rows(me), mine]
+    for group in range(4):
+        slots = range(max(group * 16 - 1, 0), group * 16 + 15)
+        await_bytes(got.at[slots[0] * 16 : slots[-1] * 16 + 16, :], rs_recv.at[group])
+        for k in slots:
+            parts[k % 2] = parts[k % 2] + got[k * 16 : (k + 1) * 16, :].astype(F32)
+    piece[...] = (parts[0] + parts[1]).astype(BF16)
+    place = out_hbm.at[rows(me), mine]
+    keep = pltpu.make_async_copy(piece, place, keep_sem.at[0])
+    keep.start()
+
+    @pl.loop(1, 64)
+    def _(k):
         copy = pltpu.make_async_remote_copy(
-            src_ref=piece, dst_ref=piece, send_sem=gather_send, recv_sem=gather_recv.at[k // 16],
+            src_ref=piece, dst_ref=place, send_sem=gather_send, recv_sem=gather_recv.at[k // 16],
             device_id=(shifted(me, k), core), device_id_type=MESH,
         )
         copy.start()
-        return carry
-
-    lax.fori_loop(1, 64, gather, 0)
-
-    backs = []
+
+    backs = [feat_keep]
+    keep.wait()
     for k in range(4):
         count = 240 if k == 0 else 256
         await_bytes(half.at[0:count, :], gather_recv.at[k])
-        block = pl.ds(pl.multiple_of(lax.rem(me // 16 + 4 - k, 4) * 256, 256), 256)
-        backs.append(send(out_ref.at[block, mine], out_ref.at[block, mine], back_sem.at[k], sibling))
-    await_bytes(late_yz, yz_sem.at[0])
-    await_bytes(late_yz, yz_sem.at[1])
-    far = late_total[...].astype(F32)
-    for k in range(15):
-        far = far + late_yz[k].astype(F32)
-    late_out_ref[rows(core), :] = far
-    backs.append(send(late_out_ref.at[rows(core), :], late_out_ref.at[rows(core), :], late_back_sem, sibling))
-    await_bytes(got, rs_sem.at[0])
+        block = out_hbm.at[pl.ds(pl.multiple_of(lax.rem(me // 16 + 4 - k, 4) * 256, 256), 256), mine]
+        backs.append(send(block, block, back_sem.at[k], sibling))
+        if k == 0:
+            await_bytes(late_yz, yz_sem.at[0])
+            await_bytes(late_yz, yz_sem.at[1])
+            far = late_total[...].astype(F32)
+            for n in range(15):
+                far = far + late_yz[n].astype(F32)
+            late_far[...] = far
+            place = late_hbm.at[rows(core), :]
+            backs.append(pltpu.make_async_copy(late_far, place, keep_sem.at[1]))
+            backs[-1].start()
+            backs.append(send(late_far, place, late_back_sem, sibling))
+    await_bytes(got, rs_send)
     await_bytes(got, gather_send)
     for sem in (far_sem.at[0], far_sem.at[1]):
         await_bytes(feat_far.at[0:3], sem)
@@ -378,8 +413,13 @@
 
 def unpack_kernel(
     sums_ref, late_ref, feat_ref,
-    features_ref, in_one_ref, in_two_hbm, out_one_ref, out_two_ref, w_one_ref, w_two_ref, in_two, feat, store_sem,
+    features_hbm, in_one_hbm, in_two_hbm, out_one_hbm, out_two_hbm, w_one_hbm, w_two_hbm,
+    features_ref, in_one_ref, in_two, out_one_ref, out_two_ref, w_one_ref, w_two_ref, feat, store_sem,
 ):
+    def store(src, dst):
+        stores.append(pltpu.make_async_copy(src, dst, store_sem.at[len(stores)]))
+        stores[-1].start()
+
     stores = []
     row = lax.broadcasted_iota(jnp.int32, (128, 128), 0)
     eye = jnp.where(row == lax.broadcasted_iota(jnp.int32, (128, 128), 1), 1.0, 0.0).astype(BF16)
@@ -394,8 +434,7 @@
             else:
                 block = dot_nt(eye, sums_ref[j * 128 : (j + 1) * 128, -k * 128 : (1 - k) * 128])
             in_two[band, j * 128 : j * 128 + width] = block[0:height, 0:width]
-        stores.append(pltpu.make_async_copy(in_two.at[band, :], in_two_hbm.at[band, :], store_sem.at[i]))
-        stores[-1].start()
+        store(in_two.at[band, :], in_two_hbm.at[band, :])
     w_two_ref[:, 0:512] = sums_ref[896:960, :].astype(F32)
     rest = sums_ref[960:1024, :].astype(F32)
     w_two_ref[:, 512:864] = rest[:, 0:352]
@@ -415,8 +454,14 @@
     for r in range(8):
         block = feat[pl.ds(r, 64, stride=8), :]
         features_ref[r * 8 : (r + 1) * 8, 0, :, :] = dot_nt(eye, block.astype(BF16)).reshape(8, 16, 64).astype(BF16)
-    for store in stores:
-        store.wait()
+    store(w_two_ref, w_two_hbm)
+    store(out_two_ref, out_two_hbm)
+    store(in_one_ref, in_one_hbm)
+    store(w_one_ref, w_one_hbm)
+    store(out_one_ref, out_one_hbm)
+    store(features_ref, features_hbm)
+    for copy in stores:
+        copy.wait()
 
 
 def local(volume, kernel_one, kernel_two, cotangent):
@@ -428,7 +473,7 @@
         name="step",
         out_shape=(shape((1024, 512), BF16), shape((32, 256), F32), shape((4, 128, 128), BF16)),
         in_specs=[pl.BlockSpec(memory_space=pl.ANY)] * 5,
-        out_specs=(VM,) * 3,
+        out_specs=(pl.BlockSpec(memory_space=pl.ANY),) * 3,
         scratch_shapes=[
             buf((4, 1, 4, 128, 128), BF16), buf((32, 108), BF16), buf((64, 864), BF16), buf((64, 1024), BF16),
             buf((128, 384), F32), dma((5,)),
@@ -439,11 +484,11 @@
             buf((4, 128, 128), BF16), buf((1024, 512), BF16), buf((64, 1024), BF16),
             buf((864, 128), F32), buf((3, 128, 256), BF16), buf((2, 256, 1024), BF16),
             buf((4, 128, 128), BF16), buf((128, 1024), BF16), buf((64, 1024), BF16),
-            buf((1024, 256), BF16), buf((1024, 256), BF16), buf((1008, 256), BF16),
+            buf((1024, 256), BF16), buf((1024, 256), BF16), buf((1008, 256), BF16), buf((16, 256), BF16),
             buf((32, 256), BF16), buf((16, 256), BF16), buf((3, 16, 256), BF16), buf((16, 256), BF16),
-            buf((15, 16, 256), BF16), buf((16, 256), BF16),
-            dma((2,)), dma((2,)), dma((2,)), dma((2,)), dma((2,)), dma((2,)), dma((2,)), dma((2,)), dma((2,)), dma((2,)),
-            dma, dma((4,)), dma((4, 2)), dma((2,)),
+            buf((15, 16, 256), BF16), buf((16, 256), BF16), buf((16, 256), F32),
+            dma((2,)), dma((2,)), dma((2,)), dma((2, 2)), dma((2,)), dma, dma((4,)), dma((2,)), dma((2,)), dma((2,)),
+            dma((2,)), dma, dma((4,)), dma((4, 2)), dma((2,)), dma((3,)),
         ],
         compiler_params=pltpu.CompilerParams(
             vmem_limit_bytes=VMEM_CAP, collective_id=0, has_side_effects=True
@@ -457,8 +502,11 @@
             shape((64, 64), F32), shape((32, 108), F32), shape((64, 864), F32),
         ),
         in_specs=[VM] * 3,
-        out_specs=(VM, VM, pl.BlockSpec(memory_space=pl.ANY), VM, VM, VM, VM),
-        scratch_shapes=[buf((864, 864), F32), buf((512, 128), F32), dma((7,))],
+        out_specs=(pl.BlockSpec(memory_space=pl.ANY),) * 7,
+        scratch_shapes=[
+            buf((64, 1, 16, 64), BF16), buf((108, 108), F32), buf((864, 864), F32), buf((32, 32), F32),
+            buf((64, 64), F32), buf((32, 108), F32), buf((64, 864), F32), buf((512, 128), F32), dma((13,)),
+        ],
         compiler_params=pltpu.CompilerParams(vmem_limit_bytes=VMEM_CAP),
     )(sums, late, feat)
     return features.transpose(0, 1, 3, 2), in_one, in_two, out_one, out_two, w_one.T, w_two.T

time: 54 us -> 53.5 us (level)
    pallas_call x1, Pallas kernels: 4.02 us -> 3.44 us  [local(): pl.pallas_call(unpack_kernel, name='unpack', out_shape=(shape((64, 1, 16,...]
where the time goes in v5:
time: 53.5 us; the launch traced here: 53.4 us
  Pallas kernels  52.8 us (99%)
  between operations  0.64 us (1%)
    pallas_call x1, Pallas kernels, local(): pl.pallas_call(step_kernel, name='step', out_shape=(shape((1024, 512), BF...  49.3 us
    pallas_call x1, Pallas kernels, local(): pl.pallas_call(unpack_kernel, name='unpack', out_shape=(shape((64, 1, 16,...  3.44 us

profile of v5, /device:TPU:1, one launch (start us, length us, event | category | flops | bytes accessed | tf_op | source)
XLA Modules:
  0.0 53.4 jit_solution(17347603812685409143)
XLA Ops:
  0.6 49.3 %step.1 = (bf16[1024,512]{1,0:T(8,128)(2,1)}, f32[32,256]{1,0:T(8,128)}, bf16[4,128,128]{2,1,0:T(8,128)(2,1)}) custom-call(bf16[4,1,4,128,128]{4,3,2,1,0:T(8,128)(2,1)} %vol_hbm.1, bf16[32,108]{1,0:T(8,128)(2,1)} %bitcast.8, bf16[64,864]{1,0:T(8,128)(2,1)} %bitcast.7, bf16[64,1024]{1,0:T(8,128)(2,1)} %bitcast.6, f32[128,384]{1,0:T(8,128)} %constant.2.clone.tap_hbm), custom_call_target="tpu_custom_call" | custom-call | tf_op jit(solution)/shard_map/step/pallas_call | solution.py:471
  49.9 3.4 %unpack.1 = (bf16[64,1,16,64]{3,2,1,0:T(8,128)(2,1)}, f32[108,108]{1,0:T(8,128)}, f32[864,864]{1,0:T(8,128)}, f32[32,32]{1,0:T(8,128)}, f32[64,64]{1,0:T(8,128)}, /*index=5*/f32[32,108]{1,0:T(8,128)}, f32[64,864]{1,0:T(8,128)}) custom-call(bf16[1024,512]{1,0:T(8,128)(2,1)} %get-tuple-element.17.sums_ref, f32[32,256]{1,0:T(8,128)} %get-tuple-element.18.late_ref, ...), custom_call_target="tpu_custom_call" | custom-call | tf_op jit(solution)/shard_map/unpack/pallas_call | solution.py:497

commit v6 on v5

--- a/solution.py
+++ b/solution.py
@@ -122,8 +122,8 @@
         tiles[:, k * 128 : (k + 1) * 128] = total[k * 32 : (k + 1) * 32, :]
 
 
-def group_matrix(half_tile, pick):
-    lane = lax.broadcasted_iota(jnp.int32, (128, 128), 0) - half_tile * 64
+def group_matrix(pick):
+    lane = lax.broadcasted_iota(jnp.int32, (128, 128), 0)
     col = lax.broadcasted_iota(jnp.int32, (128, 128), 1)
     for low in range(8):
         inside = (col >= low * 16) & (col < (low + 1) * 16)
@@ -231,7 +231,7 @@
     backward_weights(k2_ref, k2f, aa)
     pre_two[...] = layer_two_part(aa, 2, hid[...])
 
-    group_matrix((me // 4) & 1, pick)
+    group_matrix(pick)
 
     rim_copy.wait()
     spread_planes(
@@ -250,17 +250,20 @@
     g2[...] = (cot_ref[...].astype(F32) * (1.0 / math.sqrt(TOTAL_TWO)) * slope).astype(BF16)
     g2_copy = send(g2, g2_in, g2_sem, below)
 
-    feat[...] = act.astype(BF16)
+    act = act.astype(BF16).astype(F32)
     plane = me // 4
-    half_tile = plane & 1
+    left = lax.broadcasted_iota(jnp.int32, (1, 128), 1) < 64
+    for tile in range(8):
+        low, high = act[0:32, tile * 128 : (tile + 1) * 128], act[32:64, tile * 128 : (tile + 1) * 128]
+        feat[2 * tile] = jnp.where(left, low, pltpu.roll(high, 64, 1)).astype(BF16)
+        feat[2 * tile + 1] = jnp.where(left, pltpu.roll(low, 64, 1), high).astype(BF16)
 
     @pl.loop(1, 16)
     def _(k):
         to = shifted(me, 4 * k)
-        tile = pl.ds(pl.multiple_of((to // 8) * 128, 128), 128)
-        send(feat.at[:, tile], feat_near.at[plane], feat_sem, (to, core))
-
-    feat_near[plane] = feat[:, pl.ds(pl.multiple_of((me // 8) * 128, 128), 128)]
+        send(feat.at[to // 4], feat_near.at[plane], feat_sem, (to, core))
+
+    feat_near[plane] = feat[plane]
 
     place_taps(lower, 0, p2f)
     for j in range(8):
@@ -324,9 +327,15 @@
 
     for sem in (feat_sem.at[0], feat_sem.at[1]):
         await_bytes(feat_near.at[0:15], sem)
-    for k in range(16):
-        feat_mid[k * 64 : (k + 1) * 64, :] = feat_near[k].astype(F32)
-    wide = jnp.concatenate([feat_mid[pl.ds(low, 128, stride=8), :] for low in range(8)], axis=1).astype(BF16)
+    halves_wide = []
+    for side in range(2):
+        for k in range(16):
+            block = feat_near[k].astype(F32)
+            feat_mid[k * 32 : (k + 1) * 32, :] = pltpu.roll(block, 64, 1) if side else block
+        halves_wide.append(
+            jnp.concatenate([feat_mid[pl.ds(low, 64, stride=8), :] for low in range(8)], axis=1).astype(BF16)
+        )
+    wide = jnp.concatenate(halves_wide, axis=0)
     wide = dot(wide, pick[...]).astype(BF16)
     for x in range(4):
         feat_far[x] = wide[:, x * 128 : (x + 1) * 128]
@@ -448,9 +457,10 @@
     out_one_ref[...] = late[:, 128:160]
     for x in range(4):
         plane = feat_ref[x].astype(F32)
-        for yz in range(16):
-            at = (yz * 4 + x) * 8
-            feat[at : at + 8, :] = plane[yz * 8 : (yz + 1) * 8, :]
+        for side in range(2):
+            for yz in range(16):
+                at, row = (yz * 4 + x) * 8 + side * 4, side * 64 + yz * 4
+                feat[at : at + 4, :] = plane[row : row + 4, :]
     for r in range(8):
         block = feat[pl.ds(r, 64, stride=8), :]
         features_ref[r * 8 : (r + 1) * 8, 0, :, :] = dot_nt(eye, block.astype(BF16)).reshape(8, 16, 64).astype(BF16)
@@ -480,7 +490,7 @@
             buf((16, 136, 128), F32), buf((640, 512), F32), buf((4096, 128), F32), buf((640, 1024), BF16),
             buf((512, 640), BF16), buf((128, 1536), BF16), buf((32, 128), BF16), buf((128, 384), BF16),
             buf((256, 1024), F32), buf((128, 1024), BF16), buf((64, 1024), F32), buf((8, 864, 128), F32), buf((1280, 1024), BF16),
-            buf((32, 512), F32), buf((1024, 512), BF16), buf((64, 1024), BF16), buf((16, 64, 128), BF16), buf((1024, 128), F32),
+            buf((32, 512), F32), buf((1024, 512), BF16), buf((16, 32, 128), BF16), buf((16, 32, 128), BF16), buf((512, 128), F32),
             buf((4, 128, 128), BF16), buf((1024, 512), BF16), buf((64, 1024), BF16),
             buf((864, 128), F32), buf((3, 128, 256), BF16), buf((2, 256, 1024), BF16),
             buf((4, 128, 128), BF16), buf((128, 1024), BF16), buf((64, 1024), BF16),

time: 53.5 us -> 52.9 us (0.989)
  Pallas kernels: 52.8 us -> 52.1 us
    pallas_call x1, Pallas kernels: 49.3 us -> 48.6 us  [local(): pl.pallas_call(step_kernel, name='step', out_shape=(shape((1024, 512), BF...]
where the time goes in v6:
time: 52.9 us; the launch traced here: 52.7 us
  Pallas kernels  52.1 us (98%)
  between operations  0.64 us (1%)
    pallas_call x1, Pallas kernels, local(): pl.pallas_call(step_kernel, name='step', out_shape=(shape((1024, 512), BF...  48.6 us
    pallas_call x1, Pallas kernels, local(): pl.pallas_call(unpack_kernel, name='unpack', out_shape=(shape((64, 1, 16,...  3.45 us

profile of v6, /device:TPU:1, one launch (start us, length us, event | category | flops | bytes accessed | tf_op | source)
XLA Modules:
  0.0 52.7 jit_solution(2200854776983446887)
XLA Ops:
  0.6 48.6 %step.1 = (bf16[1024,512]{1,0:T(8,128)(2,1)}, f32[32,256]{1,0:T(8,128)}, bf16[4,128,128]{2,1,0:T(8,128)(2,1)}) custom-call(bf16[4,1,4,128,128]{4,3,2,1,0:T(8,128)(2,1)} %vol_hbm.1, bf16[32,108]{1,0:T(8,128)(2,1)} %bitcast.8, bf16[64,864]{1,0:T(8,128)(2,1)} %bitcast.7, bf16[64,1024]{1,0:T(8,128)(2,1)} %bitcast.6, f32[128,384]{1,0:T(8,128)} %constant.2.clone.tap_hbm), custom_call_target="tpu_custom_call" | custom-call | tf_op jit(solution)/shard_map/step/pallas_call | solution.py:481
  49.3 3.4 %unpack.1 = (bf16[64,1,16,64]{3,2,1,0:T(8,128)(2,1)}, f32[108,108]{1,0:T(8,128)}, f32[864,864]{1,0:T(8,128)}, f32[32,32]{1,0:T(8,128)}, f32[64,64]{1,0:T(8,128)}, /*index=5*/f32[32,108]{1,0:T(8,128)}, f32[64,864]{1,0:T(8,128)}) custom-call(bf16[1024,512]{1,0:T(8,128)(2,1)} %get-tuple-element.17.sums_ref, f32[32,256]{1,0:T(8,128)} %get-tuple-element.18.late_ref, ...), custom_call_target="tpu_custom_call" | custom-call | tf_op jit(solution)/shard_map/unpack/pallas_call | solution.py:507

commit v7 on v6

--- a/solution.py
+++ b/solution.py
@@ -389,19 +389,20 @@
     @pl.loop(1, 64)
     def _(k):
         copy = pltpu.make_async_remote_copy(
-            src_ref=piece, dst_ref=place, send_sem=gather_send, recv_sem=gather_recv.at[k // 16],
+            src_ref=piece, dst_ref=place, send_sem=gather_send, recv_sem=gather_recv.at[k // 4],
             device_id=(shifted(me, k), core), device_id_type=MESH,
         )
         copy.start()
 
     backs = [feat_keep]
     keep.wait()
-    for k in range(4):
-        count = 240 if k == 0 else 256
+    for k in range(16):
+        count = 48 if k == 0 else 64
         await_bytes(half.at[0:count, :], gather_recv.at[k])
-        block = out_hbm.at[pl.ds(pl.multiple_of(lax.rem(me // 16 + 4 - k, 4) * 256, 256), 256), mine]
+        line = shifted(me, ((4 - k // 4) % 4) * 16 + ((4 - k % 4) % 4) * 4) // 4
+        block = out_hbm.at[rows(line, 64), mine]
         backs.append(send(block, block, back_sem.at[k], sibling))
-        if k == 0:
+        if k == 3:
             await_bytes(late_yz, yz_sem.at[0])
             await_bytes(late_yz, yz_sem.at[1])
             far = late_total[...].astype(F32)
@@ -498,7 +499,7 @@
             buf((32, 256), BF16), buf((16, 256), BF16), buf((3, 16, 256), BF16), buf((16, 256), BF16),
             buf((15, 16, 256), BF16), buf((16, 256), BF16), buf((16, 256), F32),
             dma((2,)), dma((2,)), dma((2,)), dma((2, 2)), dma((2,)), dma, dma((4,)), dma((2,)), dma((2,)), dma((2,)),
-            dma((2,)), dma, dma((4,)), dma((4, 2)), dma((2,)), dma((3,)),
+            dma((2,)), dma, dma((16,)), dma((16, 2)), dma((2,)), dma((3,)),
         ],
         compiler_params=pltpu.CompilerParams(
             vmem_limit_bytes=VMEM_CAP, collective_id=0, has_side_effects=True

time: 52.9 us -> 53.2 us (level)
  no operation moved by 1% of the time
where the time goes in v7:
time: 53.2 us; the launch traced here: 53 us
  Pallas kernels  52.4 us (98%)
  between operations  0.64 us (1%)
    pallas_call x1, Pallas kernels, local(): pl.pallas_call(step_kernel, name='step', out_shape=(shape((1024, 512), BF...  48.9 us
    pallas_call x1, Pallas kernels, local(): pl.pallas_call(unpack_kernel, name='unpack', out_shape=(shape((64, 1, 16,...  3.45 us

profile of v7, /device:TPU:1, one launch (start us, length us, event | category | flops | bytes accessed | tf_op | source)
XLA Modules:
  0.0 53.0 jit_solution(4125776530591787061)
XLA Ops:
  0.6 48.9 %step.1 = (bf16[1024,512]{1,0:T(8,128)(2,1)}, f32[32,256]{1,0:T(8,128)}, bf16[4,128,128]{2,1,0:T(8,128)(2,1)}) custom-call(bf16[4,1,4,128,128]{4,3,2,1,0:T(8,128)(2,1)} %vol_hbm.1, bf16[32,108]{1,0:T(8,128)(2,1)} %bitcast.8, bf16[64,864]{1,0:T(8,128)(2,1)} %bitcast.7, bf16[64,1024]{1,0:T(8,128)(2,1)} %bitcast.6, f32[128,384]{1,0:T(8,128)} %constant.2.clone.tap_hbm), custom_call_target="tpu_custom_call" | custom-call | tf_op jit(solution)/shard_map/step/pallas_call | solution.py:482
  49.6 3.5 %unpack.1 = (bf16[64,1,16,64]{3,2,1,0:T(8,128)(2,1)}, f32[108,108]{1,0:T(8,128)}, f32[864,864]{1,0:T(8,128)}, f32[32,32]{1,0:T(8,128)}, f32[64,64]{1,0:T(8,128)}, /*index=5*/f32[32,108]{1,0:T(8,128)}, f32[64,864]{1,0:T(8,128)}) custom-call(bf16[1024,512]{1,0:T(8,128)(2,1)} %get-tuple-element.17.sums_ref, f32[32,256]{1,0:T(8,128)} %get-tuple-element.18.late_ref, ...), custom_call_target="tpu_custom_call" | custom-call | tf_op jit(solution)/shard_map/unpack/pallas_call | solution.py:508
